TPU v7x, 32 devices: a whole 2x2x4 slice. The times are simulated.
32 devices in a mesh: dp: 1, loop: 16 (over z, y, x), head: 2 (over core).
Axes of the slice: x: 2, y: 2, z: 4, core: 2. Of those that a mesh axis runs over, the one named last changes fastest.
Arguments:
- query_embed: bfloat16 [65536, 256], P(('dp', 'loop', 'head')), may hold values from -3 to 3
- query_heads: bfloat16 [65536, 256], P(('dp', 'loop'), 'head'), may hold values from -7 to 7
- voxel_kv: bfloat16 [32768, 512], P(('dp', 'loop'), 'head'), may hold values from -7 to 7
- band_start: int32 [1024], P(('dp', 'loop')), may hold values from 0 to 255, as said below
- band_count: int32 [1024], P(('dp', 'loop')), may hold values from 2 to 4, as said below
- out_weight: bfloat16 [256, 256], replicated, may hold values from -0.375 to 0.375
- norm_gain: float32 [256], replicated, may hold values from 0.5 to 1.5
Outputs:
- refined: bfloat16 [65536, 256], P(('dp', 'loop', 'head'))
Inputs may be any that keep to these rules, and one draw needn't show every extreme that they name: Query block b attends band_count[b] voxel blocks; in every draw some 64 cyclically consecutive query blocks all have the count 4, and so do the first and the last query block of every run of 64 blocks that starts at a multiple of 64. Query block b attends voxel blocks (band_start[b] + j) mod 256 for 0 <= j < band_count[b]; each of them lies at a cyclic distance of at most 3 blocks from block 16 * b // 64. For b a multiple of 64 the band starts exactly 3 blocks before that block; for b + 1 a multiple of 64 it starts exactly 1 block before that block.
All inputs are finite; a program needn't handle non-finite values.
Results may differ from a plain program's by a relative error of at most 0.008.
Values may be sent and summed in bfloat16 or wider, within the bound.
A program may use at most 64 MiB of HBM per device.

v0:
```python
from functools import reduce

import jax
import jax.numpy as jnp
from jax import lax
from jax.sharding import PartitionSpec as P

HEAD_DIM = 32
MOST = 4
REACH = 3


def passed_along(value, axis, steps):
    count = lax.axis_size(axis)
    pairs = [(source, (source + steps) % count) for source in range(count)]
    return lax.ppermute(value, axis, pairs)


def for_sending(x):
    return jax.tree.map(lambda a: a.astype(jnp.bfloat16) if a.dtype == jnp.float32 else a, x)


def attend_span(query_rows, rel_start, counts, kv_rows, modulus):
    width = query_rows.shape[1]
    heads_here = width // HEAD_DIM
    row_count = query_rows.shape[0]
    query_blocks = row_count // 64
    block_total = kv_rows.shape[0] // 128
    span = MOST
    per_super = 8
    supers = query_blocks // per_super
    score_scale = HEAD_DIM ** (-0.5)
    signed = jnp.where(rel_start >= modulus - span, rel_start - modulus, rel_start).astype(
        jnp.int32
    )
    clamped = jnp.clip(signed, -span, block_total)
    padded = jnp.pad(kv_rows, ((span * 128, span * 128), (0, 0)))
    offsets = jnp.arange(span, dtype=jnp.int32)

    def one_block(queries, start_here, begin, length):
        window = lax.dynamic_slice_in_dim(padded, (begin + span) * 128, span * 128, 0)
        block_ids = begin + offsets
        relative = block_ids - start_here
        live = (block_ids >= 0) & (block_ids < block_total) & (relative >= 0) & (relative < length)
        live_rows = jnp.repeat(live, 128)
        numer_list = []
        peak_list = []
        total_list = []
        for head in range(heads_here):
            query_part = queries[:, head * HEAD_DIM : (head + 1) * HEAD_DIM]
            key_part = window[:, 2 * head * HEAD_DIM : (2 * head + 1) * HEAD_DIM]
            value_part = window[:, (2 * head + 1) * HEAD_DIM : (2 * head + 2) * HEAD_DIM]
            scores = (
                lax.dot_general(
                    query_part,
                    key_part,
                    (((1,), (1,)), ((), ())),
                    preferred_element_type=jnp.float32,
                )
                * score_scale
            )
            scores = jnp.where(live_rows[None, :], scores, -1e30)
            peak = jnp.max(scores, axis=1)
            weights = jnp.where(live_rows[None, :], jnp.exp(scores - peak[:, None]), 0.0)
            total_list.append(jnp.sum(weights, axis=1))
            peak_list.append(peak)
            numer_list.append(
                jnp.dot(
                    weights.astype(jnp.bfloat16), value_part, preferred_element_type=jnp.float32
                )
            )
        return (
            jnp.concatenate(numer_list, axis=1),
            jnp.stack(peak_list, axis=1),
            jnp.stack(total_list, axis=1),
        )

    def one_super(operands):
        queries, start_row, begin_row, length_row = operands
        return jax.vmap(one_block)(queries, start_row, begin_row, length_row)

    query_split = query_rows.reshape(supers, per_super, 64, width)
    numerator, running_max, denominator = lax.map(
        one_super,
        (
            query_split,
            signed.reshape(supers, per_super),
            clamped.reshape(supers, per_super),
            counts.reshape(supers, per_super),
        ),
    )
    numerator = numerator.reshape(row_count, width)
    running_max = running_max.reshape(row_count, heads_here)
    denominator = denominator.reshape(row_count, heads_here)
    return (numerator, running_max, denominator)


def combine_parts(partials):
    overall = reduce(jnp.maximum, [entry[1] for entry in partials])
    numerator = jnp.zeros_like(partials[0][0])
    denominator = jnp.zeros_like(partials[0][2])
    for entry in partials:
        factor = jnp.exp(entry[1] - overall)
        numerator = numerator + entry[0] * jnp.repeat(factor, HEAD_DIM, axis=1)
        denominator = denominator + entry[2] * factor
    return (numerator, denominator)


def widen_rows(partial_value, before, after):
    numerator, running_max, denominator = partial_value
    numerator = jnp.pad(numerator, ((before, after), (0, 0)))
    running_max = jnp.pad(running_max, ((before, after), (0, 0)), constant_values=-1e30)
    denominator = jnp.pad(denominator, ((before, after), (0, 0)))
    return (numerator, running_max, denominator)


def local(query_embed, query_heads, voxel_kv, band_start, band_count, out_weight, norm_gain):
    loop_size = lax.axis_size("loop")
    shard_index = lax.axis_index("loop")
    vblocks_here = voxel_kv.shape[0] // 128
    qblocks_here = query_heads.shape[0] // 64
    all_vblocks = vblocks_here * loop_size
    first_block = shard_index * vblocks_here
    edge_blocks = min(
        qblocks_here, ((REACH * qblocks_here + vblocks_here - 1) // vblocks_here + 7) // 8 * 8
    )
    plans = [(qblocks_here - edge_blocks, edge_blocks, 1), (0, edge_blocks, -1)]
    partials = [
        attend_span(
            query_heads,
            jnp.mod(band_start - first_block, all_vblocks),
            band_count,
            voxel_kv,
            all_vblocks,
        )
    ]
    for first_edge, edge_width, direction in plans:
        edge_rows = query_heads[first_edge * 64 : (first_edge + edge_width) * 64]
        edge_starts = band_start[first_edge : first_edge + edge_width]
        edge_counts = band_count[first_edge : first_edge + edge_width]
        guests = passed_along((edge_rows, edge_starts, edge_counts), "loop", direction)
        visiting = attend_span(
            guests[0],
            jnp.mod(guests[1] - first_block, all_vblocks),
            guests[2],
            voxel_kv,
            all_vblocks,
        )
        coming = passed_along(
            (for_sending(visiting[0]), for_sending(visiting[1]), for_sending(visiting[2])),
            "loop",
            -direction,
        )
        after_rows = (qblocks_here - first_edge - edge_width) * 64
        partials.append(widen_rows(coming, first_edge * 64, after_rows))
    numerator, denominator = combine_parts(partials)
    attended = (numerator / jnp.repeat(denominator, HEAD_DIM, axis=1)).astype(jnp.bfloat16)
    row_features = lax.all_to_all(attended, "head", split_axis=0, concat_axis=1, tiled=True)
    projected = jnp.dot(row_features, out_weight, preferred_element_type=jnp.float32)
    mixed = query_embed.astype(jnp.float32) + projected
    centred = mixed - jnp.mean(mixed, axis=1, keepdims=True)
    variance = jnp.mean(centred * centred, axis=1, keepdims=True)
    refined = centred * lax.rsqrt(variance + 1e-05) * norm_gain
    return refined.astype(jnp.bfloat16)


def solution(mesh):
    placed = (
        P(("dp", "loop", "head"), None),
        P(("dp", "loop"), "head"),
        P(("dp", "loop"), "head"),
        P(("dp", "loop")),
        P(("dp", "loop")),
        P(),
        P(),
    )
    return jax.shard_map(
        local,
        mesh=mesh,
        in_specs=placed,
        out_specs=P(("dp", "loop", "head"), None),
        check_vma=False,
    )
```

profile of v0, /device:TPU:0, one launch (start us, length us, event | category | flops | bytes accessed | tf_op | source)
XLA Modules:
  0.0 403.6 jit_solution(11400371208419964355)
XLA Ops:
  0.8 2.9 collective-permute-start
  3.7 4.0 collective-permute-start.4
  10.1 5.2 %collective-permute-start.6 = (bf16[1024,128]{1,0:T(8,128)(2,1)S(1)}, bf16[1024,128]{1,0:T(8,128)(2,1)S(1)}, u32[]{:S(2)}, u32[]{:S(2)}) collective-permute-start(bf16[1024,128]{1,0:T(8,128)(2,1)S(1)} %get-tuple-element.448), channel_id=1, source_target_pairs={{0,30},{2,0},{4,2},{6,4},{8,6},{10,8},{12,10},{14,12},{16,14},{18,... | collective-permute-start | bytes 786440 | tf_op jit(solution)/shard_map/ppermute | solution.py:16
  20.0 2.1 collective-permute-start.5
  23.8 47.5 %while.57 = (s32[]{:T(128)}, bf16[2,8,64,128]{3,2,1,0:T(8,128)(2,1)S(1)}, bf16[2,8,64,4]{2,1,3,0:T(8,128)(2,1)S(1)}, bf16[2,8,64,4]{2,3,1,0:T(4,128)(2,1)S(1)}, ...) while((s32[]{:T(128)}, ...), condition=%wide.region_19.20_spmd.clone, body=%wide.region_10.19_spmd.clone.sunk | while | flops 144208208 | bytes 26477884 | solution.py:83
  23.9 16.5 %while.61 = (s32[]{:T(128)}, bf16[3072,256]{1,0:T(8,128)(2,1)S(1)}, s32[8,2]{0,1:T(2,128)S(1)}, bf16[8,512,256]{1,2,0:T(8,128)(2,1)}, s32[]{:T(128)}) while((s32[]{:T(128)}, bf16[3072,256]{1,0:T(8,128)(2,1)S(1)}, s32[8,2]{0,1:T(2,128)S(1)}, bf16[8,512,256]{1,2,0:T(8,128)(2,1)}, s32[]{:T(128)}) %tuple.182), condition=%wide.while_cond.1, body=%wide.while_body.1.sunk | while | flops 2 | bytes 1573469 | solution.py:41
  47.7 16.5 %while.61 = (s32[]{:T(128)}, bf16[3072,256]{1,0:T(8,128)(2,1)S(1)}, s32[8,2]{0,1:T(2,128)S(1)}, bf16[8,512,256]{1,2,0:T(8,128)(2,1)}, s32[]{:T(128)}) while((s32[]{:T(128)}, bf16[3072,256]{1,0:T(8,128)(2,1)S(1)}, s32[8,2]{0,1:T(2,128)S(1)}, bf16[8,512,256]{1,2,0:T(8,128)(2,1)}, s32[]{:T(128)}) %tuple.182), condition=%wide.while_cond.1, body=%wide.while_body.1.sunk | while | flops 2 | bytes 1573469 | solution.py:41
  71.4 5.6 %collective-permute-start.10 = (bf16[1024,4]{0,1:T(4,128)(2,1)S(1)}, bf16[1024,4]{0,1:T(4,128)(2,1)}, u32[]{:S(2)}, u32[]{:S(2)}) collective-permute-start(bf16[1024,4]{0,1:T(4,128)(2,1)S(1)} %convert_element_type.131), channel_id=1, source_target_pairs={{0,30},{2,0},{4,2},{6,4},{8,6},{10,8},{12,10},{14,12},{16,14},{18,... | collective-permute-start | bytes 24584 | tf_op jit(solution)/shard_map/ppermute | solution.py:16
  77.1 47.5 %while.59 = (s32[]{:T(128)}, bf16[2,8,64,128]{3,2,1,0:T(8,128)(2,1)S(1)}, bf16[2,8,64,4]{2,1,3,0:T(8,128)(2,1)S(1)}, bf16[2,8,64,4]{2,3,1,0:T(4,128)(2,1)S(1)}, ...) while((s32[]{:T(128)}, ...), condition=%wide.region_29.30_spmd.clone, body=%wide.region_20.29_spmd.clone.sunk | while | flops 144208208 | bytes 26477884 | solution.py:83
  77.3 16.5 %while.62 = (s32[]{:T(128)}, bf16[3072,256]{1,0:T(8,128)(2,1)S(1)}, s32[8,2]{0,1:T(2,128)S(1)}, bf16[8,512,256]{1,2,0:T(8,128)(2,1)}, s32[]{:T(128)}) while((s32[]{:T(128)}, bf16[3072,256]{1,0:T(8,128)(2,1)S(1)}, s32[8,2]{0,1:T(2,128)S(1)}, bf16[8,512,256]{1,2,0:T(8,128)(2,1)}, s32[]{:T(128)}) %tuple.179), condition=%wide.while_cond.2, body=%wide.while_body.2.sunk | while | flops 2 | bytes 1573469 | solution.py:41
  101.0 16.5 %while.62 = (s32[]{:T(128)}, bf16[3072,256]{1,0:T(8,128)(2,1)S(1)}, s32[8,2]{0,1:T(2,128)S(1)}, bf16[8,512,256]{1,2,0:T(8,128)(2,1)}, s32[]{:T(128)}) while((s32[]{:T(128)}, bf16[3072,256]{1,0:T(8,128)(2,1)S(1)}, s32[8,2]{0,1:T(2,128)S(1)}, bf16[8,512,256]{1,2,0:T(8,128)(2,1)}, s32[]{:T(128)}) %tuple.179), condition=%wide.while_cond.2, body=%wide.while_body.2.sunk | while | flops 2 | bytes 1573469 | solution.py:41
  125.4 5.6 %collective-permute-start.3 = (bf16[1024,4]{0,1:T(4,128)(2,1)}, bf16[1024,4]{0,1:T(4,128)(2,1)}, u32[]{:S(2)}, u32[]{:S(2)}) collective-permute-start(bf16[1024,4]{0,1:T(4,128)(2,1)} %convert_element_type.119), channel_id=1, source_target_pairs={{0,30},{2,0},{4,2},{6,4},{8,6},{10,8},{12,10},{14,12},{16,14},{18,... | collective-permute-start | bytes 24584 | tf_op jit(solution)/shard_map/ppermute | solution.py:16
  131.7 231.4 %while.55 = (s32[]{:T(128)}, f32[8,8,64,128]{3,2,1,0:T(8,128)}, f32[8,8,64,4]{2,1,0,3:T(8,128)}, f32[8,8,64,4]{2,1,0,3:T(8,128)}, s32[8,8]{1,0:T(8,128)}, /*inde...) while((s32[]{:T(128)}, f32[8,8,64,128]{3,2,1,0:T(8,128)}, ...), condition=%wide.region_9.10_spmd.clone, body=%wide.region_0.9_spmd.clone.sunk | while | flops 143860048 | bytes 27412788 | solution.py:83
  134.7 16.8 %while.60 = (s32[]{:T(128)}, bf16[3072,256]{1,0:T(8,128)(2,1)S(1)}, s32[8,2]{0,1:T(2,128)S(1)}, bf16[8,512,256]{1,2,0:T(8,128)(2,1)}, s32[]{:T(128)}) while((s32[]{:T(128)}, bf16[3072,256]{1,0:T(8,128)(2,1)S(1)}, s32[8,2]{0,1:T(2,128)S(1)}, bf16[8,512,256]{1,2,0:T(8,128)(2,1)}, s32[]{:T(128)}) %tuple.185), condition=%wide.while_cond, body=%wide.while_body.sunk | while | flops 2 | bytes 1573469 | solution.py:41
  163.6 16.8 %while.60 = (s32[]{:T(128)}, bf16[3072,256]{1,0:T(8,128)(2,1)S(1)}, s32[8,2]{0,1:T(2,128)S(1)}, bf16[8,512,256]{1,2,0:T(8,128)(2,1)}, s32[]{:T(128)}) while((s32[]{:T(128)}, bf16[3072,256]{1,0:T(8,128)(2,1)S(1)}, s32[8,2]{0,1:T(2,128)S(1)}, bf16[8,512,256]{1,2,0:T(8,128)(2,1)}, s32[]{:T(128)}) %tuple.185), condition=%wide.while_cond, body=%wide.while_body.sunk | while | flops 2 | bytes 1573469 | solution.py:41
  192.5 16.8 %while.60 = (s32[]{:T(128)}, bf16[3072,256]{1,0:T(8,128)(2,1)S(1)}, s32[8,2]{0,1:T(2,128)S(1)}, bf16[8,512,256]{1,2,0:T(8,128)(2,1)}, s32[]{:T(128)}) while((s32[]{:T(128)}, bf16[3072,256]{1,0:T(8,128)(2,1)S(1)}, s32[8,2]{0,1:T(2,128)S(1)}, bf16[8,512,256]{1,2,0:T(8,128)(2,1)}, s32[]{:T(128)}) %tuple.185), condition=%wide.while_cond, body=%wide.while_body.sunk | while | flops 2 | bytes 1573469 | solution.py:41
  221.4 16.8 %while.60 = (s32[]{:T(128)}, bf16[3072,256]{1,0:T(8,128)(2,1)S(1)}, s32[8,2]{0,1:T(2,128)S(1)}, bf16[8,512,256]{1,2,0:T(8,128)(2,1)}, s32[]{:T(128)}) while((s32[]{:T(128)}, bf16[3072,256]{1,0:T(8,128)(2,1)S(1)}, s32[8,2]{0,1:T(2,128)S(1)}, bf16[8,512,256]{1,2,0:T(8,128)(2,1)}, s32[]{:T(128)}) %tuple.185), condition=%wide.while_cond, body=%wide.while_body.sunk | while | flops 2 | bytes 1573469 | solution.py:41
  250.3 16.8 %while.60 = (s32[]{:T(128)}, bf16[3072,256]{1,0:T(8,128)(2,1)S(1)}, s32[8,2]{0,1:T(2,128)S(1)}, bf16[8,512,256]{1,2,0:T(8,128)(2,1)}, s32[]{:T(128)}) while((s32[]{:T(128)}, bf16[3072,256]{1,0:T(8,128)(2,1)S(1)}, s32[8,2]{0,1:T(2,128)S(1)}, bf16[8,512,256]{1,2,0:T(8,128)(2,1)}, s32[]{:T(128)}) %tuple.185), condition=%wide.while_cond, body=%wide.while_body.sunk | while | flops 2 | bytes 1573469 | solution.py:41
  279.2 16.8 %while.60 = (s32[]{:T(128)}, bf16[3072,256]{1,0:T(8,128)(2,1)S(1)}, s32[8,2]{0,1:T(2,128)S(1)}, bf16[8,512,256]{1,2,0:T(8,128)(2,1)}, s32[]{:T(128)}) while((s32[]{:T(128)}, bf16[3072,256]{1,0:T(8,128)(2,1)S(1)}, s32[8,2]{0,1:T(2,128)S(1)}, bf16[8,512,256]{1,2,0:T(8,128)(2,1)}, s32[]{:T(128)}) %tuple.185), condition=%wide.while_cond, body=%wide.while_body.sunk | while | flops 2 | bytes 1573469 | solution.py:41
  308.1 16.8 %while.60 = (s32[]{:T(128)}, bf16[3072,256]{1,0:T(8,128)(2,1)S(1)}, s32[8,2]{0,1:T(2,128)S(1)}, bf16[8,512,256]{1,2,0:T(8,128)(2,1)}, s32[]{:T(128)}) while((s32[]{:T(128)}, bf16[3072,256]{1,0:T(8,128)(2,1)S(1)}, s32[8,2]{0,1:T(2,128)S(1)}, bf16[8,512,256]{1,2,0:T(8,128)(2,1)}, s32[]{:T(128)}) %tuple.185), condition=%wide.while_cond, body=%wide.while_body.sunk | while | flops 2 | bytes 1573469 | solution.py:41
  326.0 1.5 fusion.297
  337.0 16.8 %while.60 = (s32[]{:T(128)}, bf16[3072,256]{1,0:T(8,128)(2,1)S(1)}, s32[8,2]{0,1:T(2,128)S(1)}, bf16[8,512,256]{1,2,0:T(8,128)(2,1)}, s32[]{:T(128)}) while((s32[]{:T(128)}, bf16[3072,256]{1,0:T(8,128)(2,1)S(1)}, s32[8,2]{0,1:T(2,128)S(1)}, bf16[8,512,256]{1,2,0:T(8,128)(2,1)}, s32[]{:T(128)}) %tuple.185), condition=%wide.while_cond, body=%wide.while_body.sunk | while | flops 2 | bytes 1573469 | solution.py:41
  366.6 5.6 %collective-permute-start.8 = (bf16[1024,128]{1,0:T(8,128)(2,1)S(1)}, bf16[1024,128]{1,0:T(8,128)(2,1)S(1)}, u32[]{:S(2)}, u32[]{:S(2)}) collective-permute-start(bf16[1024,128]{1,0:T(8,128)(2,1)S(1)} %bitcast.301), channel_id=1, source_target_pairs={{0,30},{2,0},{4,2},{6,4},{8,6},{10,8},{12,10},{14,12},{16,14},{18,... | collective-permute-start | bytes 786440 | tf_op jit(solution)/shard_map/ppermute | solution.py:16
  373.1 1.5 broadcast_in_dim.234
  374.6 2.9 copy.72
  377.5 1.5 broadcast_in_dim.235
  379.1 2.9 copy.74
  382.0 1.6 broadcast_in_dim.236
  383.6 2.9 copy.76
  388.0 3.0 copy.80
  391.0 4.6 %fusion.191 = bf16[4096,128]{1,0:T(8,128)(2,1)S(1)} fusion(f32[4096,128]{1,0:T(8,128)} %copy.80, f32[4096,128]{1,0:T(8,128)} %copy.76, f32[4096,128]{1,0:T(8,128)} %copy.74, f32[4096,128]{1,0:T(8,128)} %copy.72, f32[8,8,64,128]{3,2,1,0:T(8,128)} %get-tuple-element.167, bf16[1024,128]{1,0:T(8,128)(2,1)S(1)} %collective-permute-done.9, ...), kind=kLoop, calls=%fused_computation.247 | loop fusion | flops 4718592 | bytes 12058624 | tf_op jit(solution)/shard_map/convert_element_type | solution.py:157
  396.2 4.7 %all_to_all.19 = bf16[2,2048,128]{1,2,0:T(8,128)(2,1)S(1)} all-to-all(bf16[2,2048,128]{1,2,0:T(8,128)(2,1)S(1)} %copy.81), channel_id=1, replica_groups=mesh['dp'=1,'loop'=16,'head'=2] {'head'}, dimensions={0} | all-to-all | bytes 2097152 | tf_op jit(solution)/shard_map/all_to_all | solution.py:158
  (864 shorter events, 342.4 us)
Async XLA Ops:
  0.0 400.9 %copy-start = (bf16[256,256]{1,0:T(8,128)(2,1)S(1)}, bf16[256,256]{1,0:T(8,128)(2,1)}, u32[]{:S(2)}) copy-start(bf16[256,256]{1,0:T(8,128)(2,1)} %param.18) | copy-start | bytes 393220
  0.8 19.2 %collective-permute-start = (s32[16]{0:T(128)S(1)}, s32[16]{0:T(128)S(1)}, u32[]{:S(2)}, u32[]{:S(2)}) collective-permute-start(s32[16]{0:T(128)S(1)} %get-tuple-element.451), channel_id=1, source_target_pairs={{0,2},{2,4},{4,6},{6,8},{8,10},{10,12},{12,14},{14,16},{16,18},{18... | collective-permute-start | bytes 200 | tf_op jit(solution)/shard_map/ppermute | solution.py:16
  3.7 18.3 %collective-permute-start.4 = (s32[16]{0:T(128)S(1)}, s32[16]{0:T(128)S(1)}, u32[]{:S(2)}, u32[]{:S(2)}) collective-permute-start(s32[16]{0:T(128)S(1)} %get-tuple-element.452), channel_id=1, source_target_pairs={{0,30},{2,0},{4,2},{6,4},{8,6},{10,8},{12,10},{14,12},{16,14},{18,... | collective-permute-start | bytes 200 | tf_op jit(solution)/shard_map/ppermute | solution.py:16
  8.8 14.9 %collective-permute-start.2 = (bf16[1024,128]{1,0:T(8,128)(2,1)S(1)}, bf16[1024,128]{1,0:T(8,128)(2,1)S(1)}, u32[]{:S(2)}, u32[]{:S(2)}) collective-permute-start(bf16[1024,128]{1,0:T(8,128)(2,1)S(1)} %get-tuple-element.447), channel_id=1, source_target_pairs={{0,2},{2,4},{4,6},{6,8},{8,10},{10,12},{12,14},{14,16},{16,18},{18... | collective-permute-start | bytes 786440 | tf_op jit(solution)/shard_map/ppermute | solution.py:16
  9.7 12.7 %collective-permute-start.1 = (s32[16]{0:T(128)S(1)}, s32[16]{0:T(128)S(1)}, u32[]{:S(2)}, u32[]{:S(2)}) collective-permute-start(s32[16]{0:T(128)S(1)} %get-tuple-element.449), channel_id=1, source_target_pairs={{0,2},{2,4},{4,6},{6,8},{8,10},{10,12},{12,14},{14,16},{16,18},{18... | collective-permute-start | bytes 200 | tf_op jit(solution)/shard_map/ppermute | solution.py:16
  10.1 66.9 %collective-permute-start.6 = (bf16[1024,128]{1,0:T(8,128)(2,1)S(1)}, bf16[1024,128]{1,0:T(8,128)(2,1)S(1)}, u32[]{:S(2)}, u32[]{:S(2)}) collective-permute-start(bf16[1024,128]{1,0:T(8,128)(2,1)S(1)} %get-tuple-element.448), channel_id=1, source_target_pairs={{0,30},{2,0},{4,2},{6,4},{8,6},{10,8},{12,10},{14,12},{16,14},{18,... | collective-permute-start | bytes 786440 | tf_op jit(solution)/shard_map/ppermute | solution.py:16
  20.0 3.6 collective-permute-start.5
  40.6 2.9 copy-start.1
  64.4 2.9 copy-start.1
  71.2 5.8 %copy-start.8 = (bf16[2,8,64,128]{3,2,1,0:T(8,128)(2,1)}, bf16[2,8,64,128]{3,2,1,0:T(8,128)(2,1)S(1)}, u32[]{:S(2)}) copy-start(bf16[2,8,64,128]{3,2,1,0:T(8,128)(2,1)S(1)} %get-tuple-element.171) | copy-start | bytes 786436
  71.4 300.9 %collective-permute-start.10 = (bf16[1024,4]{0,1:T(4,128)(2,1)S(1)}, bf16[1024,4]{0,1:T(4,128)(2,1)}, u32[]{:S(2)}, u32[]{:S(2)}) collective-permute-start(bf16[1024,4]{0,1:T(4,128)(2,1)S(1)} %convert_element_type.131), channel_id=1, source_target_pairs={{0,30},{2,0},{4,2},{6,4},{8,6},{10,8},{12,10},{14,12},{16,14},{18,... | collective-permute-start | bytes 24584 | tf_op jit(solution)/shard_map/ppermute | solution.py:16
  94.0 2.9 copy-start.2
  117.7 2.9 copy-start.2
  124.6 7.1 %copy-start.6 = (bf16[2,8,64,128]{3,2,1,0:T(8,128)(2,1)}, bf16[2,8,64,128]{3,2,1,0:T(8,128)(2,1)S(1)}, u32[]{:S(2)}) copy-start(bf16[2,8,64,128]{3,2,1,0:T(8,128)(2,1)S(1)} %get-tuple-element.172) | copy-start | bytes 786436
  124.7 247.5 %collective-permute-start.11 = (bf16[1024,4]{0,1:T(4,128)(2,1)S(1)}, bf16[1024,4]{0,1:T(4,128)(2,1)}, u32[]{:S(2)}, u32[]{:S(2)}) collective-permute-start(bf16[1024,4]{0,1:T(4,128)(2,1)S(1)} %convert_element_type.134), channel_id=1, source_target_pairs={{0,2},{2,4},{4,6},{6,8},{8,10},{10,12},{12,14},{14,16},{16,18},{18... | collective-permute-start | bytes 24584 | tf_op jit(solution)/shard_map/ppermute | solution.py:16
  125.4 246.8 %collective-permute-start.3 = (bf16[1024,4]{0,1:T(4,128)(2,1)}, bf16[1024,4]{0,1:T(4,128)(2,1)}, u32[]{:S(2)}, u32[]{:S(2)}) collective-permute-start(bf16[1024,4]{0,1:T(4,128)(2,1)} %convert_element_type.119), channel_id=1, source_target_pairs={{0,30},{2,0},{4,2},{6,4},{8,6},{10,8},{12,10},{14,12},{16,14},{18,... | collective-permute-start | bytes 24584 | tf_op jit(solution)/shard_map/ppermute | solution.py:16
  131.7 240.6 %collective-permute-start.7 = (bf16[1024,4]{0,1:T(4,128)(2,1)}, bf16[1024,4]{0,1:T(4,128)(2,1)}, u32[]{:S(2)}, u32[]{:S(2)}) collective-permute-start(bf16[1024,4]{0,1:T(4,128)(2,1)} %convert_element_type.122), channel_id=1, source_target_pairs={{0,2},{2,4},{4,6},{6,8},{8,10},{10,12},{12,14},{14,16},{16,18},{18... | collective-permute-start | bytes 24584 | tf_op jit(solution)/shard_map/ppermute | solution.py:16
  131.7 233.5 %copy-start.5 = (bf16[2048,256]{1,0:T(8,128)(2,1)S(1)}, bf16[2048,256]{1,0:T(8,128)(2,1)}, u32[]{:S(2)}) copy-start(bf16[2048,256]{1,0:T(8,128)(2,1)} %param.13) | copy-start | bytes 3145732
  152.6 2.9 copy-start.3
  181.5 2.9 copy-start.3
  210.4 2.9 copy-start.3
  239.3 2.9 copy-start.3
  268.2 2.9 copy-start.3
  297.1 2.9 copy-start.3
  326.0 2.9 copy-start.3
  354.9 2.9 copy-start.3
  363.1 3.5 copy-start.9
  363.1 9.1 %copy-start.7 = (bf16[2,8,64,128]{3,2,1,0:T(8,128)(2,1)S(1)}, bf16[2,8,64,128]{3,2,1,0:T(8,128)(2,1)}, u32[]{:S(2)}) copy-start(bf16[2,8,64,128]{3,2,1,0:T(8,128)(2,1)} %copy-done.6) | copy-start | bytes 786436
  366.6 24.3 %collective-permute-start.8 = (bf16[1024,128]{1,0:T(8,128)(2,1)S(1)}, bf16[1024,128]{1,0:T(8,128)(2,1)S(1)}, u32[]{:S(2)}, u32[]{:S(2)}) collective-permute-start(bf16[1024,128]{1,0:T(8,128)(2,1)S(1)} %bitcast.301), channel_id=1, source_target_pairs={{0,30},{2,0},{4,2},{6,4},{8,6},{10,8},{12,10},{14,12},{16,14},{18,... | collective-permute-start | bytes 786440 | tf_op jit(solution)/shard_map/ppermute | solution.py:16
  372.2 18.7 %collective-permute-start.9 = (bf16[1024,128]{1,0:T(8,128)(2,1)S(1)}, bf16[1024,128]{1,0:T(8,128)(2,1)S(1)}, u32[]{:S(2)}, u32[]{:S(2)}) collective-permute-start(bf16[1024,128]{1,0:T(8,128)(2,1)S(1)} %bitcast.300), channel_id=1, source_target_pairs={{0,2},{2,4},{4,6},{6,8},{8,10},{10,12},{12,14},{14,16},{16,18},{18... | collective-permute-start | bytes 786440 | tf_op jit(solution)/shard_map/ppermute | solution.py:16
  396.1 4.7 %copy-start.4 = (bf16[2048,256]{0,1:T(8,128)(2,1)S(1)}, bf16[2048,256]{0,1:T(8,128)(2,1)}, u32[]{:S(2)}) copy-start(bf16[2048,256]{0,1:T(8,128)(2,1)} %copy.61) | copy-start | bytes 3145732
  401.4 0.7 copy-start.10
where the time goes:
time: 406 us; the launch traced here: 404 us
  local copies, waits for them, and re-layouts  266 us (66%)
  matrix products  62.3 us (15%)
  other arithmetic  35 us (9%)
  starting transfers between devices  31.5 us (8%)
  blocking collectives  4.71 us (1%)
    gather x480, local copies, waits for them, and re-layouts  199 us
    dot_general x48, matrix products, one_block(): lax.dot_general(query_part, key_part, (((1,), (1,)), ((), ())), preferred...  45.2 us
    ppermute x12, starting transfers between devices, passed_along(): return lax.ppermute(value, axis, pairs)  31.5 us
    dot_general x48, matrix products, one_block(): jnp.dot(weights.astype(jnp.bfloat16), value_part, preferred_element_type=...  16.6 us
    reduce_sum x12, other arithmetic, one_block(): total_list.append(jnp.sum(weights, axis=1))  16.4 us
    dynamic_slice x24, local copies, waits for them, and re-layouts, attend_span(): lax.map(one_super, (query_split, signed.reshape(supers, per_super), clamp...  9.48 us
    reshape x3, local copies, waits for them, and re-layouts, combine_parts(): numerator = numerator + entry[0] * jnp.repeat(factor, HEAD_DIM, axis=1)  8.71 us
  transfers between devices with their start and end apart: 12, of which 1 were waited for; matrix products, arithmetic and copies ran while one was open for 88% of the time, Pallas kernels for 0%

commit v1 on v0

v1 whole, which is shorter than its diff:
```python
import functools
import math

import jax
import jax.numpy as jnp
from jax import lax
from jax.experimental import pallas as pl
from jax.experimental.pallas import tpu as pltpu
from jax.sharding import PartitionSpec as P

HEAD_DIM = 32
MOST = 4
REACH = 3
QB = 64
VB = 128
LOG_SCALE = HEAD_DIM**-0.5 * math.log2(math.e)


def prepare(kv, keys, values_t, first, count):
    lane = lax.broadcasted_iota(jnp.int32, (VB, VB), 1) // HEAD_DIM
    ones = jnp.ones((16, VB), jnp.bfloat16)

    def body(i, _):
        block = kv[pl.ds(pl.multiple_of(i * VB, VB), VB), :].astype(jnp.float32)
        low, high = block[:, :VB], block[:, VB:]
        key = jnp.where(
            lane == 0,
            low,
            jnp.where(
                lane == 1,
                pltpu.roll(low, 96, 1),
                jnp.where(lane == 2, pltpu.roll(high, 64, 1), pltpu.roll(high, 32, 1)),
            ),
        )
        value = jnp.where(
            lane == 0,
            pltpu.roll(low, 96, 1),
            jnp.where(
                lane == 1,
                pltpu.roll(low, 64, 1),
                jnp.where(lane == 2, pltpu.roll(high, 32, 1), high),
            ),
        )
        keys[pl.ds(pl.multiple_of((first + i) * VB, VB), VB), :] = key.astype(jnp.bfloat16)
        values_t[first + i, pl.ds(0, VB), :] = value.T.astype(jnp.bfloat16)
        values_t[first + i, pl.ds(VB, 16), :] = ones
        return 0

    lax.fori_loop(0, count, body, 0)


def attend_block(query, start, length, last_window, keys, values_t):
    begin = jnp.minimum(start, last_window)
    lane_head = lax.broadcasted_iota(jnp.int32, (QB, VB), 1) // HEAD_DIM
    spread = jnp.concatenate(
        [jnp.where(lane_head == h, query, jnp.zeros_like(query)) for h in range(4)], axis=0
    )
    window = keys[pl.ds(pl.multiple_of(begin * VB, VB), MOST * VB), :]
    scores = lax.dot_general(
        window, spread, (((1,), (1,)), ((), ())), preferred_element_type=jnp.float32
    )
    parts = [scores[j * VB : (j + 1) * VB] for j in range(MOST)]
    live = [
        jnp.logical_and(begin + j >= start, begin + j < start + length) for j in range(MOST)
    ]
    tops = [
        jnp.where(live[j], jnp.max(parts[j], axis=0, keepdims=True), -1e30) for j in range(MOST)
    ]
    peak = functools.reduce(jnp.maximum, tops)
    weights = jnp.concatenate(
        [
            jnp.exp2(((parts[j] - jnp.where(live[j], peak, 1e30)) * LOG_SCALE).astype(jnp.bfloat16))
            for j in range(MOST)
        ],
        axis=0,
    )
    window_t = jnp.concatenate([values_t[begin + j] for j in range(MOST)], axis=1)
    summed = jnp.dot(window_t, weights, preferred_element_type=jnp.float32)
    inverse = 1.0 / summed[VB : VB + 1, :]
    both = jnp.concatenate(
        [summed[0:64, :VB] * inverse[:, :VB], summed[64:128, VB:] * inverse[:, VB:]], axis=0
    ).T
    odd = lane_head % 2 == 1
    return jnp.where(odd, both[QB:], both[:QB]).astype(jnp.bfloat16)


def attend_kernel(starts, counts, query, left, middle, right, out, keys, values_t):
    inner = middle.shape[0] // VB
    prepare(left, keys, values_t, 0, REACH)
    prepare(middle, keys, values_t, REACH, inner)
    prepare(right, keys, values_t, REACH + inner, REACH)
    last_window = inner + 2 * REACH - MOST
    group = 4

    def body(i, _):
        for g in range(group):
            b = i * group + g
            rows = pl.ds(pl.multiple_of(b * QB, QB), QB)
            out[rows, :] = attend_block(
                query[rows, :], starts[b], counts[b], last_window, keys, values_t
            )
        return 0

    lax.fori_loop(0, query.shape[0] // QB // group, body, 0)


def local(query_embed, query_heads, voxel_kv, band_start, band_count, out_weight, norm_gain):
    loop_size = lax.axis_size("loop")
    shard_index = lax.axis_index("loop")
    vblocks = voxel_kv.shape[0] // VB
    all_vblocks = vblocks * loop_size
    halo = REACH * VB
    right = lax.ppermute(
        voxel_kv[:halo], "loop", [(s, (s - 1) % loop_size) for s in range(loop_size)]
    )
    left = lax.ppermute(
        voxel_kv[-halo:], "loop", [(s, (s + 1) % loop_size) for s in range(loop_size)]
    )
    starts = jnp.mod(band_start - shard_index * vblocks + REACH, all_vblocks)
    vmem = pl.BlockSpec(memory_space=pltpu.VMEM)
    smem = pl.BlockSpec(memory_space=pltpu.SMEM)
    attended = pl.pallas_call(
        attend_kernel,
        out_shape=jax.ShapeDtypeStruct(query_heads.shape, jnp.bfloat16),
        in_specs=[smem, smem, vmem, vmem, vmem, vmem],
        out_specs=vmem,
        scratch_shapes=[
            pltpu.VMEM(((vblocks + 2 * REACH) * VB, VB), jnp.bfloat16),
            pltpu.VMEM((vblocks + 2 * REACH, VB + 16, VB), jnp.bfloat16),
        ],
        compiler_params=pltpu.CompilerParams(vmem_limit_bytes=40 * 2**20),
    )(starts, band_count, query_heads, left, voxel_kv, right)
    row_features = lax.all_to_all(attended, "head", split_axis=0, concat_axis=1, tiled=True)
    projected = jnp.dot(row_features, out_weight, preferred_element_type=jnp.float32)
    mixed = query_embed.astype(jnp.float32) + projected
    centred = mixed - jnp.mean(mixed, axis=1, keepdims=True)
    variance = jnp.mean(centred * centred, axis=1, keepdims=True)
    refined = centred * lax.rsqrt(variance + 1e-05) * norm_gain
    return refined.astype(jnp.bfloat16)


def solution(mesh):
    placed = (
        P(("dp", "loop", "head"), None),
        P(("dp", "loop"), "head"),
        P(("dp", "loop"), "head"),
        P(("dp", "loop")),
        P(("dp", "loop")),
        P(),
        P(),
    )
    return jax.shard_map(
        local,
        mesh=mesh,
        in_specs=placed,
        out_specs=P(("dp", "loop", "head"), None),
        check_vma=False,
    )
```

time: 406 us -> 61 us (0.15)
  local copies, waits for them, and re-layouts: 266 us -> 7.33 us
  matrix products: 62.3 us -> 0.5 us
  other arithmetic: 35 us -> 0.53 us
  Pallas kernels: 0 us -> 33.1 us
  starting transfers between devices: 31.5 us -> 7 us
  waiting for transfers between devices: 1.11 us -> 7.68 us
    gather x480 -> x0, local copies, waits for them, and re-layouts: 199 us -> none
    dot_general x96 -> x0, matrix products: 61.8 us -> none  [the longest x48 45.2 us: one_block(): lax.dot_general(query_part, key_part, (((1,), (1,)), ((), ())), preferred...]
    pallas_call x0 -> x1, Pallas kernels: none -> 33.1 us  [local(): pl.pallas_call(attend_kernel, out_shape=jax.ShapeDtypeStruct(query_heads....]
    ppermute x12 -> x2, starting transfers between devices: 31.5 us -> 7 us  [the longest x1 6.99 us: local(): lax.ppermute(voxel_kv[:halo], 'loop', [(s, (s - 1) % loop_size) for s in...]
    reshape x15 -> x0, local copies, waits for them, and re-layouts: 16.9 us -> none  [the longest x3 8.71 us: combine_parts(): numerator = numerator + entry[0] * jnp.repeat(factor, HEAD_DIM, axis=1)]
    reduce_sum x12 -> x0, other arithmetic: 16.4 us -> none  [one_block(): total_list.append(jnp.sum(weights, axis=1))]
    dynamic_slice x24 -> x0, local copies, waits for them, and re-layouts: 9.48 us -> none  [attend_span(): lax.map(one_super, (query_split, signed.reshape(supers, per_super), clamp...]
    dynamic_update_slice x24 -> x0, local copies, waits for them, and re-layouts: 7.93 us -> none  [attend_span(): lax.map(one_super, (query_split, signed.reshape(supers, per_super), clamp...]
  transfers between devices with their start and end apart: 12 -> 2, of which waited for: 1 -> 2; matrix products, arithmetic and copies ran while one was open for 88% -> 4% of each run, Pallas kernels for 0% -> 0%
where the time goes in v1:
time: 61 us; the launch traced here: 60.8 us
  Pallas kernels  33.1 us (54%)
  waiting for transfers between devices  7.68 us (13%)
  local copies, waits for them, and re-layouts  7.33 us (12%)
  starting transfers between devices  7 us (11%)
  blocking collectives  4.58 us (8%)
    pallas_call x1, Pallas kernels, local(): pl.pallas_call(attend_kernel, out_shape=jax.ShapeDtypeStruct(query_heads....  33.1 us
    ppermute x1, starting transfers between devices, local(): lax.ppermute(voxel_kv[:halo], 'loop', [(s, (s - 1) % loop_size) for s in...  6.99 us
    ppermute x1, waiting for transfers between devices, local(): lax.ppermute(voxel_kv[-halo:], 'loop', [(s, (s + 1) % loop_size) for s in...  5.8 us
    all_to_all x1, blocking collectives, local(): lax.all_to_all(attended, 'head', split_axis=0, concat_axis=1, tiled=True)  4.58 us
    unnamed x19, local copies, waits for them, and re-layouts  4.29 us
    ppermute x1, waiting for transfers between devices, local(): lax.ppermute(voxel_kv[:halo], 'loop', [(s, (s - 1) % loop_size) for s in...  1.88 us
    convert_element_type x1, local copies, waits for them, and re-layouts, local(): return refined.astype(jnp.bfloat16)  1.31 us
  transfers between devices with their start and end apart: 2, of which 2 were waited for; matrix products, arithmetic and copies ran while one was open for 4% of the time, Pallas kernels for 0%

profile of v1, /device:TPU:0, one launch (start us, length us, event | category | flops | bytes accessed | tf_op | source)
XLA Modules:
  0.0 60.8 jit_solution(16482807555054770530)
XLA Ops:
  0.0 0.0 copy-start
  0.0 0.0 copy-start.1
  0.0 0.0 copy-start.8
  0.0 0.0 copy-start.5
  0.0 0.0 copy-start.2
  0.0 1.2 %fusion.1 = (bf16[384,256]{1,0:T(8,128)(2,1)S(1)}, bf16[384,256]{1,0:T(8,128)(2,1)S(1)}) fusion(bf16[2048,256]{1,0:T(8,128)(2,1)} %middle.1), kind=kLoop, calls=%fused_computation.9 | loop fusion | bytes 786432 | tf_op jit(solution)/shard_map/slice | solution.py:114
  1.2 7.0 %collective-permute-start.1 = (bf16[384,256]{1,0:T(8,128)(2,1)S(1)}, bf16[384,256]{1,0:T(8,128)(2,1)S(1)}, u32[]{:S(2)}, u32[]{:S(2)}) collective-permute-start(bf16[384,256]{1,0:T(8,128)(2,1)S(1)} %get-tuple-element.5), channel_id=1, source_target_pairs={{0,30},{2,0},{4,2},{6,4},{8,6},{10,8},{12,10},{14,12},{16,14},{18,... | collective-permute-start | bytes 589832 | tf_op jit(solution)/shard_map/ppermute | solution.py:113
  8.2 0.0 collective-permute-start
  8.2 2.3 %copy.10 = bf16[2048,256]{0,1:T(8,128)(2,1)} copy(bf16[2048,256]{1,0:T(8,128)(2,1)} %param.7) | data formatting | bytes 2097152 | tf_op args[0]
  10.5 0.0 copy-done.8
  10.5 1.9 %collective-permute-done.1.right = bf16[384,256]{1,0:T(8,128)(2,1)S(1)} collective-permute-done((bf16[384,256]{1,0:T(8,128)(2,1)S(1)}, bf16[384,256]{1,0:T(8,128)(2,1)S(1)}, u32[]{:S(2)}, u32[]{:S(2)}) %collective-permute-start.1) | collective-permute-done | bytes 196640 | tf_op jit(solution)/shard_map/ppermute | solution.py:113
  12.4 5.8 %collective-permute-done.left = bf16[384,256]{1,0:T(8,128)(2,1)S(1)} collective-permute-done((bf16[384,256]{1,0:T(8,128)(2,1)S(1)}, bf16[384,256]{1,0:T(8,128)(2,1)S(1)}, u32[]{:S(2)}, u32[]{:S(2)}) %collective-permute-start) | collective-permute-done | bytes 196640 | tf_op jit(solution)/shard_map/ppermute | solution.py:116
  18.2 0.0 copy-start.3
  18.2 0.7 %copy-done.3 = bf16[384,256]{1,0:T(8,128)(2,1)} copy-done((bf16[384,256]{1,0:T(8,128)(2,1)}, bf16[384,256]{1,0:T(8,128)(2,1)S(1)}, u32[]{:S(2)}) %copy-start.3) | copy-done | bytes 196632
  18.8 0.0 copy-done.1
  18.8 0.0 copy-done.5
  18.9 0.0 copy-done.2
  18.9 0.0 copy-start.4
  18.9 0.9 %copy-done.4 = bf16[384,256]{1,0:T(8,128)(2,1)S(1)} copy-done((bf16[384,256]{1,0:T(8,128)(2,1)S(1)}, bf16[384,256]{1,0:T(8,128)(2,1)}, u32[]{:S(2)}) %copy-start.4) | copy-done | bytes 196632
  19.8 33.1 %shard_map.73 = bf16[4096,128]{1,0:T(8,128)(2,1)S(1)} custom-call(s32[64]{0:T(128)S(1)} %and_select_fusion.starts, s32[64]{0:T(128)S(1)} %copy-done.5, bf16[4096,128]{1,0:T(8,128)(2,1)S(1)} %copy-done.2, bf16[384,256]{1,0:T(8,128)(2,1)S(1)} %copy-done.4, bf16[2048,256]{1,0:T(8,128)(2,1)S(1)} %copy-done.1, bf16[384,256]{1,0:T(8,128)(2,1)S(1)} %collective-permute-done.1.right), custom_call_target="tpu_custom_call" | custom-call | tf_op jit(solution)/shard_map/pallas_call | solution.py:122
  52.9 0.0 copy-start.6
  52.9 0.5 copy.11
  53.5 4.6 %all_to_all.19 = bf16[2,2048,128]{1,2,0:T(8,128)(2,1)S(1)} all-to-all(bf16[2,2048,128]{1,2,0:T(8,128)(2,1)S(1)} %copy.11), channel_id=1, replica_groups=mesh['dp'=1,'loop'=16,'head'=2] {'head'}, dimensions={0} | all-to-all | bytes 2097152 | tf_op jit(solution)/shard_map/all_to_all | solution.py:133
  58.0 0.0 copy-done
  58.0 0.0 copy-done.6
  58.0 0.5 fusion.2
  58.6 0.0 copy-start.7
  58.6 0.2 multiply_reduce_fusion
  58.8 0.4 copy-done.7
  59.2 0.3 multiply_convert_fusion
  59.5 1.3 %copy.12 = bf16[2048,256]{1,0:T(8,128)(2,1)} copy(bf16[2048,256]{0,1:T(8,128)(2,1)S(1)} %multiply_convert_fusion) | data formatting | bytes 2097152 | tf_op jit(solution)/shard_map/convert_element_type | solution.py:139
  (3 shorter events, 0.0 us)
Async XLA Ops:
  0.0 58.0 %copy-start = (bf16[256,256]{1,0:T(8,128)(2,1)S(1)}, bf16[256,256]{1,0:T(8,128)(2,1)}, u32[]{:S(2)}) copy-start(bf16[256,256]{1,0:T(8,128)(2,1)} %param.12) | copy-start | bytes 393220
  0.0 18.8 %copy-start.1 = (bf16[2048,256]{1,0:T(8,128)(2,1)S(1)}, bf16[2048,256]{1,0:T(8,128)(2,1)}, u32[]{:S(2)}) copy-start(bf16[2048,256]{1,0:T(8,128)(2,1)} %middle.1) | copy-start | bytes 3145732
  0.0 10.5 %copy-start.8 = (s32[64]{0:T(128)S(1)}, s32[64]{0:T(128)}, u32[]{:S(2)}) copy-start(s32[64]{0:T(128)} %param.10) | copy-start | bytes 772
  0.0 18.8 %copy-start.5 = (s32[64]{0:T(128)S(1)}, s32[64]{0:T(128)}, u32[]{:S(2)}) copy-start(s32[64]{0:T(128)} %counts.1) | copy-start | bytes 772
  0.0 18.8 %copy-start.2 = (bf16[4096,128]{1,0:T(8,128)(2,1)S(1)}, bf16[4096,128]{1,0:T(8,128)(2,1)}, u32[]{:S(2)}) copy-start(bf16[4096,128]{1,0:T(8,128)(2,1)} %query.1) | copy-start | bytes 3145732
  1.2 11.2 %collective-permute-start.1 = (bf16[384,256]{1,0:T(8,128)(2,1)S(1)}, bf16[384,256]{1,0:T(8,128)(2,1)S(1)}, u32[]{:S(2)}, u32[]{:S(2)}) collective-permute-start(bf16[384,256]{1,0:T(8,128)(2,1)S(1)} %get-tuple-element.5), channel_id=1, source_target_pairs={{0,30},{2,0},{4,2},{6,4},{8,6},{10,8},{12,10},{14,12},{16,14},{18,... | collective-permute-start | bytes 589832 | tf_op jit(solution)/shard_map/ppermute | solution.py:113
  8.2 10.0 %collective-permute-start = (bf16[384,256]{1,0:T(8,128)(2,1)S(1)}, bf16[384,256]{1,0:T(8,128)(2,1)S(1)}, u32[]{:S(2)}, u32[]{:S(2)}) collective-permute-start(bf16[384,256]{1,0:T(8,128)(2,1)S(1)} %get-tuple-element.6), channel_id=1, source_target_pairs={{0,2},{2,4},{4,6},{6,8},{8,10},{10,12},{12,14},{14,16},{16,18},{18... | collective-permute-start | bytes 589832 | tf_op jit(solution)/shard_map/ppermute | solution.py:116
  18.2 0.7 %copy-start.3 = (bf16[384,256]{1,0:T(8,128)(2,1)}, bf16[384,256]{1,0:T(8,128)(2,1)S(1)}, u32[]{:S(2)}) copy-start(bf16[384,256]{1,0:T(8,128)(2,1)S(1)} %collective-permute-done.left) | copy-start | bytes 589828
  18.9 0.9 %copy-start.4 = (bf16[384,256]{1,0:T(8,128)(2,1)S(1)}, bf16[384,256]{1,0:T(8,128)(2,1)}, u32[]{:S(2)}) copy-start(bf16[384,256]{1,0:T(8,128)(2,1)} %copy-done.3) | copy-start | bytes 589828
  52.9 5.1 %copy-start.6 = (bf16[2048,256]{0,1:T(8,128)(2,1)S(1)}, bf16[2048,256]{0,1:T(8,128)(2,1)}, u32[]{:S(2)}) copy-start(bf16[2048,256]{0,1:T(8,128)(2,1)} %copy.10) | copy-start | bytes 3145732
  58.6 0.7 %copy-start.7 = (f32[256]{0:T(256)S(1)}, f32[256]{0:T(256)}, u32[]{:S(2)}) copy-start(f32[256]{0:T(256)} %param.13) | copy-start | bytes 3076

commit v2 on v1

v2 whole, which is shorter than its diff:
```python
import functools
import math

import jax
import jax.numpy as jnp
from jax import lax
from jax.experimental import pallas as pl
from jax.experimental.pallas import tpu as pltpu
from jax.sharding import PartitionSpec as P

HEAD_DIM = 32
MOST = 4
REACH = 3
QB = 64
VB = 128
LOG_SCALE = HEAD_DIM**-0.5 * math.log2(math.e)
BF16 = jnp.bfloat16
F32 = jnp.float32


def store_values_t(block, targets):
    turned = block.T
    ones = jnp.ones((16, VB), BF16)
    for ref, index in targets:
        for h in range(4):
            ref[index + (pl.ds(h * HEAD_DIM, HEAD_DIM),)] = turned[
                (2 * h + 1) * HEAD_DIM : (2 * h + 2) * HEAD_DIM
            ]
        ref[index + (pl.ds(VB, 16),)] = ones


def scores_of(query, begin, load_window):
    lane_head = lax.broadcasted_iota(jnp.int32, (QB, VB), 1) // HEAD_DIM
    zero = jnp.zeros_like(query)
    at_0 = lane_head == 0
    at_2 = lane_head == 2
    first = [jnp.where(at_0, query, zero), jnp.where(at_2, pltpu.roll(query, 32, 1), zero)]
    second = [
        jnp.where(at_0, pltpu.roll(query, 64, 1), zero),
        jnp.where(at_2, pltpu.roll(query, 96, 1), zero),
    ]
    spread = jnp.concatenate(
        [
            jnp.concatenate(first + [zero, zero], axis=0),
            jnp.concatenate([zero, zero] + second, axis=0),
        ],
        axis=1,
    )
    return lax.dot_general(
        load_window(begin), spread, (((1,), (1,)), ((), ())), preferred_element_type=F32
    )


def finish(scores, start, begin, length, load_values):
    parts = [scores[j * VB : (j + 1) * VB] for j in range(MOST)]
    ahead = jnp.full((1, scores.shape[1]), begin - start, jnp.int32)
    many = jnp.full((1, scores.shape[1]), length, jnp.int32)
    live = [jnp.logical_and(ahead + j >= 0, ahead + j < many) for j in range(MOST)]
    tops = [
        jnp.where(live[j], jnp.max(parts[j], axis=0, keepdims=True), -1e30) for j in range(MOST)
    ]
    peak = functools.reduce(jnp.maximum, tops)
    weights = jnp.concatenate(
        [
            jnp.exp2(((parts[j] - jnp.where(live[j], peak, 1e30)) * LOG_SCALE).astype(BF16))
            for j in range(MOST)
        ],
        axis=0,
    )
    window_t = jnp.concatenate([load_values(begin + j) for j in range(MOST)], axis=1)
    summed = jnp.dot(window_t, weights, preferred_element_type=F32)
    inverse = 1.0 / summed[VB : VB + 1, :]
    both = jnp.concatenate(
        [summed[0:64, :VB] * inverse[:, :VB], summed[64:128, VB:] * inverse[:, VB:]], axis=0
    ).T
    lane_head = lax.broadcasted_iota(jnp.int32, (QB, VB), 1) // HEAD_DIM
    return jnp.where(lane_head % 2 == 1, both[QB:], both[:QB]).astype(BF16)


def attend(first, count, offset, blocks, unroll, bands, query, slots, load_window, load_values, out):
    starts, counts = bands

    def query_rows(b):
        return query[pl.ds(pl.multiple_of((first + b) * QB, QB), QB), :]

    def place(b):
        start = starts[first + b] - offset
        return start, jnp.minimum(jnp.maximum(start, 0), blocks - MOST)

    slots[0][...] = scores_of(query_rows(0), place(0)[1], load_window)

    def body(i, _):
        for g in range(2 * unroll):
            b = 2 * unroll * i + g
            after = jnp.minimum(b + 1, count - 1)
            slots[1 - g % 2][...] = scores_of(query_rows(after), place(after)[1], load_window)
            start, begin = place(b)
            out[pl.ds(pl.multiple_of(b * QB, QB), QB), :] = finish(
                slots[g % 2][...], start, begin, counts[first + b], load_values
            )
        return 0

    lax.fori_loop(0, count // (2 * unroll), body, 0)


def prepare(count, load_block, values_t):
    def body(i, _):
        store_values_t(load_block(i), [(values_t, (i,))])
        return 0

    lax.fori_loop(0, count, body, 0, unroll=True)


def rows_of(i, count, size):
    return pl.ds(pl.multiple_of(i * size, size), count * size)


def mid_kernel(starts, counts, query_hbm, kv, other, own, query, values_t, score_a, score_b, sem):
    copy = pltpu.make_async_copy(query_hbm, query, sem)
    copy.start()
    vblocks, qblocks = kv.shape[0] // VB, query.shape[0] // QB
    edge_q = qblocks // vblocks * REACH
    mid_q = qblocks // 2 - edge_q
    head = lax.axis_index("head")
    prepare(vblocks, lambda i: kv[rows_of(i, 1, VB), :], values_t)
    copy.wait()
    for side, out in ((1 - head, other), (head, own)):
        attend(
            edge_q + side * mid_q, mid_q, REACH, vblocks, 5, (starts, counts), query,
            (score_a, score_b), lambda begin: kv[rows_of(begin, MOST, VB), :],
            lambda block: values_t[block], out,
        )


def edge_kernel(
    starts, counts, query_hbm, kv_hbm, left, right, other, own,
    query, kv_edge, values_t, score_a, score_b, sems,
):
    halo, rows = left.shape[0], kv_hbm.shape[0]
    vblocks, qblocks = rows // VB, query.shape[0] // QB
    edge_q = qblocks // vblocks * REACH
    near = 2 * halo
    last = (qblocks - edge_q) * QB
    copies = [
        pltpu.make_async_copy(left, kv_edge.at[0, pl.ds(0, halo)], sems.at[0]),
        pltpu.make_async_copy(
            kv_hbm.at[pl.ds(0, near)], kv_edge.at[0, pl.ds(halo, near)], sems.at[1]
        ),
        pltpu.make_async_copy(
            kv_hbm.at[pl.ds(rows - near, near)], kv_edge.at[1, pl.ds(0, near)], sems.at[2]
        ),
        pltpu.make_async_copy(right, kv_edge.at[1, pl.ds(near, halo)], sems.at[3]),
        pltpu.make_async_copy(
            query_hbm.at[pl.ds(0, edge_q * QB)], query.at[pl.ds(0, edge_q * QB)], sems.at[4]
        ),
        pltpu.make_async_copy(
            query_hbm.at[pl.ds(last, edge_q * QB)], query.at[pl.ds(last, edge_q * QB)], sems.at[5]
        ),
    ]
    for copy in copies:
        copy.start()
    for copy in copies:
        copy.wait()
    head = lax.axis_index("head")
    for side in range(2):
        prepare(3 * REACH, lambda i: kv_edge[side, rows_of(i, 1, VB), :], values_t.at[side])
    for side, out in ((1 - head, other), (head, own)):
        attend(
            side * (qblocks - edge_q), edge_q, side * (vblocks - REACH), 3 * REACH, 3,
            (starts, counts), query, (score_a, score_b),
            lambda begin: kv_edge[side, rows_of(begin, MOST, VB), :],
            lambda block: values_t[side, block], out,
        )


def project_kernel(
    own_mid, got_mid, own_edge, got_edge, embed_hbm, weight, gain, out_hbm, embed, result, sems
):
    copy = pltpu.make_async_copy(embed_hbm, embed, sems.at[0])
    copy.start()
    head = lax.axis_index("head")
    weights = jnp.concatenate(
        [weight[rows_of(head, 1, VB), :], weight[rows_of(1 - head, 1, VB), :]], axis=0
    )
    gains = gain[...]
    tile = 256
    copy.wait()
    sends = []
    mid, edge = own_mid.shape[0], own_edge.shape[0]
    for own, got, first in (
        (own_mid, got_mid, (1 - head) * edge),
        (own_edge, got_edge, head * mid),
    ):
        for i in range(own.shape[0] // tile):
            here = slice(i * tile, (i + 1) * tile)
            there = pl.ds(pl.multiple_of(first + i * tile, tile), tile)
            features = jnp.concatenate([own[here, :], got[here, :]], axis=1)
            mixed = embed[there, :].astype(F32) + jnp.dot(
                features, weights, preferred_element_type=F32
            )
            centred = mixed - jnp.mean(mixed, axis=1, keepdims=True)
            variance = jnp.mean(centred * centred, axis=1, keepdims=True)
            result[there, :] = (centred * lax.rsqrt(variance + 1e-5) * gains).astype(BF16)
            send = pltpu.make_async_copy(
                result.at[there], out_hbm.at[there], sems.at[1 + len(sends)]
            )
            send.start()
            sends.append(send)
    for send in sends:
        send.wait()


def local(query_embed, query_heads, voxel_kv, band_start, band_count, out_weight, norm_gain):
    loop_size = lax.axis_size("loop")
    me = lax.axis_index("loop")
    vblocks, qblocks = voxel_kv.shape[0] // VB, query_heads.shape[0] // QB
    halo = REACH * VB
    edge_rows = qblocks // vblocks * REACH * QB
    mid_rows = query_heads.shape[0] // 2 - edge_rows
    vmem = pl.BlockSpec(memory_space=pltpu.VMEM)
    smem = pl.BlockSpec(memory_space=pltpu.SMEM)
    hbm = pl.BlockSpec(memory_space=pl.ANY)
    ring = range(loop_size)
    right = lax.ppermute(voxel_kv[:halo], "loop", [(s, (s - 1) % loop_size) for s in ring])
    left = lax.ppermute(voxel_kv[-halo:], "loop", [(s, (s + 1) % loop_size) for s in ring])
    starts = jnp.mod(band_start - me * vblocks + REACH, vblocks * loop_size)
    params = pltpu.CompilerParams(vmem_limit_bytes=40 * 2**20)
    query_scratch = pltpu.VMEM(query_heads.shape, BF16)
    slots = [pltpu.VMEM((MOST * VB, 4 * QB), F32)] * 2

    def cost(rows):
        return pl.CostEstimate(
            flops=rows * 2**19, bytes_accessed=rows * 2**10, transcendentals=rows * 2**11
        )

    other_mid, own_mid = pl.pallas_call(
        mid_kernel,
        out_shape=[jax.ShapeDtypeStruct((mid_rows, VB), BF16)] * 2,
        in_specs=[smem, smem, hbm, vmem],
        out_specs=[vmem, vmem],
        scratch_shapes=[
            query_scratch, pltpu.VMEM((vblocks, VB + 16, VB), BF16), *slots,
            pltpu.SemaphoreType.DMA,
        ],
        compiler_params=params,
        cost_estimate=cost(2 * mid_rows),
    )(starts, band_count, query_heads, voxel_kv)
    swap = [(0, 1), (1, 0)]
    got_mid = lax.ppermute(other_mid, "head", swap)
    other_edge, own_edge = pl.pallas_call(
        edge_kernel,
        out_shape=[jax.ShapeDtypeStruct((edge_rows, VB), BF16)] * 2,
        in_specs=[smem, smem, hbm, hbm, hbm, hbm],
        out_specs=[vmem, vmem],
        scratch_shapes=[
            query_scratch,
            pltpu.VMEM((2, 3 * halo, voxel_kv.shape[1]), BF16),
            pltpu.VMEM((2, 3 * REACH, VB + 16, VB), BF16),
            *slots,
            pltpu.SemaphoreType.DMA((6,)),
        ],
        compiler_params=params,
        cost_estimate=cost(2 * edge_rows),
    )(starts, band_count, query_heads, voxel_kv, left, right)
    got_edge = lax.ppermute(other_edge, "head", swap)
    return pl.pallas_call(
        project_kernel,
        out_shape=jax.ShapeDtypeStruct(query_embed.shape, BF16),
        in_specs=[vmem, vmem, vmem, vmem, hbm, vmem, vmem],
        out_specs=hbm,
        scratch_shapes=[
            pltpu.VMEM(query_embed.shape, BF16),
            pltpu.VMEM(query_embed.shape, BF16),
            pltpu.SemaphoreType.DMA((1 + query_embed.shape[0] // 256,)),
        ],
        compiler_params=params,
    )(own_mid, got_mid, own_edge, got_edge, query_embed, out_weight, norm_gain.reshape(1, -1))


def solution(mesh):
    placed = (
        P(("dp", "loop", "head"), None),
        P(("dp", "loop"), "head"),
        P(("dp", "loop"), "head"),
        P(("dp", "loop")),
        P(("dp", "loop")),
        P(),
        P(),
    )
    return jax.shard_map(
        local,
        mesh=mesh,
        in_specs=placed,
        out_specs=P(("dp", "loop", "head"), None),
        check_vma=False,
    )
```

time: 61 us -> 35.2 us (0.58)
  Pallas kernels: 33.1 us -> 20.7 us
  waiting for transfers between devices: 7.68 us -> 1.08 us
  blocking collectives: 4.58 us -> 0 us
  local copies, waits for them, and re-layouts: 7.33 us -> 5.48 us
    pallas_call x1 -> x3, Pallas kernels: 33.1 us -> 20.7 us  [the longest x1 10.7 us: local(): pl.pallas_call(mid_kernel, out_shape=[jax.ShapeDtypeStruct((mid_rows, VB)...]
    ppermute x1, waiting for transfers between devices: 5.8 us -> 0.01 us  [local(): lax.ppermute(voxel_kv[-halo:], 'loop', [(s, (s + 1) % loop_size) for s in...]
    all_to_all x1 -> x0, blocking collectives: 4.58 us -> none  [local(): lax.all_to_all(attended, 'head', split_axis=0, concat_axis=1, tiled=True)]
    ppermute x1, waiting for transfers between devices: 1.88 us -> 0.01 us  [local(): lax.ppermute(voxel_kv[:halo], 'loop', [(s, (s - 1) % loop_size) for s in...]
    convert_element_type x1 -> x0, local copies, waits for them, and re-layouts: 1.31 us -> none  [local(): return refined.astype(jnp.bfloat16)]
    ppermute x0 -> x2, waiting for transfers between devices: none -> 1.07 us  [the longest x1 1.07 us: local(): got_edge = lax.ppermute(other_edge, 'head', swap)]
    ppermute x0 -> x2, starting transfers between devices: none -> 0.61 us  [the longest x1 0.54 us: local(): got_edge = lax.ppermute(other_edge, 'head', swap)]
    unnamed x19 -> x14, local copies, waits for them, and re-layouts: 4.29 us -> 4.43 us
  transfers between devices with their start and end apart: 2 -> 4, of which waited for: 2 -> 1; matrix products, arithmetic and copies ran while one was open for 4% -> 0% of each run, Pallas kernels for 0% -> 54%
where the time goes in v2:
time: 35.2 us; the launch traced here: 34.9 us
  Pallas kernels  20.7 us (59%)
  starting transfers between devices  7.6 us (22%)
  local copies, waits for them, and re-layouts  5.48 us (16%)
  waiting for transfers between devices  1.08 us (3%)
    pallas_call x1, Pallas kernels, local(): pl.pallas_call(mid_kernel, out_shape=[jax.ShapeDtypeStruct((mid_rows, VB)...  10.7 us
    pallas_call x1, Pallas kernels, local(): pl.pallas_call(edge_kernel, out_shape=[jax.ShapeDtypeStruct((edge_rows, V...  8.26 us
    ppermute x1, starting transfers between devices, local(): lax.ppermute(voxel_kv[:halo], 'loop', [(s, (s - 1) % loop_size) for s in...  6.98 us
    unnamed x14, local copies, waits for them, and re-layouts  4.43 us
    pallas_call x1, Pallas kernels, local(): pl.pallas_call(project_kernel, out_shape=jax.ShapeDtypeStruct(query_embed...  1.78 us
    ppermute x1, waiting for transfers between devices, local(): got_edge = lax.ppermute(other_edge, 'head', swap)  1.07 us
    slice x1, local copies, waits for them, and re-layouts, local(): voxel_kv[:halo]  1.05 us
  transfers between devices with their start and end apart: 4, of which 1 were waited for; matrix products, arithmetic and copies ran while one was open for 0% of the time, Pallas kernels for 54%

profile of v2, /device:TPU:0, one launch (start us, length us, event | category | flops | bytes accessed | tf_op | source)
XLA Modules:
  0.0 34.9 jit_solution(4024865524865357116)
XLA Ops:
  0.0 1.0 %fusion.1 = (bf16[384,256]{1,0:T(8,128)(2,1)S(1)}, bf16[384,256]{1,0:T(8,128)(2,1)S(1)}) fusion(bf16[2048,256]{1,0:T(8,128)(2,1)} %kv_hbm.1), kind=kLoop, calls=%fused_computation.4 | loop fusion | bytes 786432 | tf_op jit(solution)/shard_map/slice | solution.py:224
  1.1 7.0 %collective-permute-start.2 = (bf16[384,256]{1,0:T(8,128)(2,1)S(1)}, bf16[384,256]{1,0:T(8,128)(2,1)S(1)}, u32[]{:S(2)}, u32[]{:S(2)}) collective-permute-start(bf16[384,256]{1,0:T(8,128)(2,1)S(1)} %get-tuple-element.13), channel_id=1, source_target_pairs={{0,30},{2,0},{4,2},{6,4},{8,6},{10,8},{12,10},{14,12},{16,14},{18,... | collective-permute-start | bytes 589832 | tf_op jit(solution)/shard_map/ppermute | solution.py:224
  8.0 0.0 collective-permute-start.1
  8.0 0.0 copy-start.6
  8.0 0.7 %copy-done.6 = s32[64]{0:T(128)S(1)} copy-done((s32[64]{0:T(128)S(1)}, s32[64]{0:T(128)}, u32[]{:S(2)}) %copy-start.6) | copy-done | bytes 280
  8.7 0.0 copy-start.5
  8.7 0.6 %copy-done.5 = s32[64]{0:T(128)S(1)} copy-done((s32[64]{0:T(128)S(1)}, s32[64]{0:T(128)}, u32[]{:S(2)}) %copy-start.5) | copy-done | bytes 280
  9.4 0.0 copy-start.1
  9.4 1.2 %copy-done.1 = bf16[2048,256]{1,0:T(8,128)(2,1)S(1)} copy-done((bf16[2048,256]{1,0:T(8,128)(2,1)S(1)}, bf16[2048,256]{1,0:T(8,128)(2,1)}, u32[]{:S(2)}) %copy-start.1) | copy-done | bytes 1048600
  10.6 0.0 copy-start.4
  10.6 1.2 %copy-done.4 = bf16[4096,128]{1,0:T(8,128)(2,1)S(1)} copy-done((bf16[4096,128]{1,0:T(8,128)(2,1)S(1)}, bf16[4096,128]{1,0:T(8,128)(2,1)}, u32[]{:S(2)}) %copy-start.4) | copy-done | bytes 1048600
  11.8 10.7 %shard_map.73 = (bf16[1280,128]{1,0:T(8,128)(2,1)S(1)}, bf16[1280,128]{1,0:T(8,128)(2,1)S(1)}) custom-call(s32[64]{0:T(128)S(1)} %and_select_fusion.starts, s32[64]{0:T(128)S(1)} %copy-done.5, bf16[4096,128]{1,0:T(8,128)(2,1)S(1)} %copy-done.4, bf16[2048,256]{1,0:T(8,128)(2,1)S(1)} %copy-done.1), custom_call_target="tpu_custom_call" | custom-call | flops 1342177280 | bytes 2621440 | tf_op jit(solution)/shard_map/pallas_call | solution.py:236
  22.5 0.0 copy-start
  22.5 0.0 copy-start.2
  22.5 0.1 collective-permute-start
  22.6 0.0 collective-permute-done.2.right
  22.6 0.0 collective-permute-done.1.left
  22.6 8.3 %shard_map.74 = (bf16[768,128]{1,0:T(8,128)(2,1)S(1)}, bf16[768,128]{1,0:T(8,128)(2,1)S(1)}) custom-call(s32[64]{0:T(128)S(1)} %and_select_fusion.starts, s32[64]{0:T(128)S(1)} %copy-done.5, bf16[4096,128]{1,0:T(8,128)(2,1)S(1)} %copy-done.4, bf16[2048,256]{1,0:T(8,128)(2,1)S(1)} %copy-done.1, bf16[384,256]{1,0:T(8,128)(2,1)S(1)} %collective-permute-done.1.left, ...), custom_call_target="tpu_custom_call" | custom-call | flops 805306368 | bytes 1572864 | tf_op jit(solution)/shard_map/pallas_call | solution.py:250
  30.9 0.5 %collective-permute-start.3 = (bf16[768,128]{1,0:T(8,128)(2,1)S(1)}, bf16[768,128]{1,0:T(8,128)(2,1)S(1)}, u32[]{:S(2)}, u32[]{:S(2)}) collective-permute-start(bf16[768,128]{1,0:T(8,128)(2,1)S(1)} %get-tuple-element.12), channel_id=1, source_target_pairs={{0,1},{1,0},{2,3},{3,2},{4,5},{5,4},{6,7},{7,6},{8,9},{9,8},{10,11... | collective-permute-start | bytes 589832 | tf_op jit(solution)/shard_map/ppermute | solution.py:265
  31.4 0.0 collective-permute-done.got_mid
  31.4 1.1 %collective-permute-done.3.got_edge = bf16[768,128]{1,0:T(8,128)(2,1)S(1)} collective-permute-done((bf16[768,128]{1,0:T(8,128)(2,1)S(1)}, bf16[768,128]{1,0:T(8,128)(2,1)S(1)}, u32[]{:S(2)}, u32[]{:S(2)}) %collective-permute-start.3) | collective-permute-done | bytes 196640 | tf_op jit(solution)/shard_map/ppermute | solution.py:265
  32.5 0.0 copy-start.3
  32.5 0.0 copy-done
  32.5 0.0 copy-done.2
  32.5 0.7 %copy-done.3 = f32[256]{0:T(256)S(1)} copy-done((f32[256]{0:T(256)S(1)}, f32[256]{0:T(256)}, u32[]{:S(2)}) %copy-start.3) | copy-done | bytes 1048
  33.2 1.8 %shard_map.75 = bf16[2048,256]{1,0:T(8,128)(2,1)} custom-call(bf16[1280,128]{1,0:T(8,128)(2,1)S(1)} %get-tuple-element.9.own_mid, bf16[1280,128]{1,0:T(8,128)(2,1)S(1)} %collective-permute-done.got_mid, bf16[768,128]{1,0:T(8,128)(2,1)S(1)} %get-tuple-element.11.own_edge, bf16[768,128]{1,0:T(8,128)(2,1)S(1)} %collective-permute-done.3.got_edge, ...), custom_call_target="tpu_custom_call" | custom-call | tf_op jit(solution)/shard_map/pallas_call | solution.py:266
  (1 shorter events, 0.0 us)
Async XLA Ops:
  1.1 21.5 %collective-permute-start.2 = (bf16[384,256]{1,0:T(8,128)(2,1)S(1)}, bf16[384,256]{1,0:T(8,128)(2,1)S(1)}, u32[]{:S(2)}, u32[]{:S(2)}) collective-permute-start(bf16[384,256]{1,0:T(8,128)(2,1)S(1)} %get-tuple-element.13), channel_id=1, source_target_pairs={{0,30},{2,0},{4,2},{6,4},{8,6},{10,8},{12,10},{14,12},{16,14},{18,... | collective-permute-start | bytes 589832 | tf_op jit(solution)/shard_map/ppermute | solution.py:224
  8.0 14.6 %collective-permute-start.1 = (bf16[384,256]{1,0:T(8,128)(2,1)S(1)}, bf16[384,256]{1,0:T(8,128)(2,1)S(1)}, u32[]{:S(2)}, u32[]{:S(2)}) collective-permute-start(bf16[384,256]{1,0:T(8,128)(2,1)S(1)} %get-tuple-element.14), channel_id=1, source_target_pairs={{0,2},{2,4},{4,6},{6,8},{8,10},{10,12},{12,14},{14,16},{16,18},{18... | collective-permute-start | bytes 589832 | tf_op jit(solution)/shard_map/ppermute | solution.py:225
  8.0 0.7 %copy-start.6 = (s32[64]{0:T(128)S(1)}, s32[64]{0:T(128)}, u32[]{:S(2)}) copy-start(s32[64]{0:T(128)} %param.10) | copy-start | bytes 772
  8.7 0.7 %copy-start.5 = (s32[64]{0:T(128)S(1)}, s32[64]{0:T(128)}, u32[]{:S(2)}) copy-start(s32[64]{0:T(128)} %counts.3) | copy-start | bytes 772
  9.4 1.2 %copy-start.1 = (bf16[2048,256]{1,0:T(8,128)(2,1)S(1)}, bf16[2048,256]{1,0:T(8,128)(2,1)}, u32[]{:S(2)}) copy-start(bf16[2048,256]{1,0:T(8,128)(2,1)} %kv_hbm.1) | copy-start | bytes 3145732
  10.6 1.2 %copy-start.4 = (bf16[4096,128]{1,0:T(8,128)(2,1)S(1)}, bf16[4096,128]{1,0:T(8,128)(2,1)}, u32[]{:S(2)}) copy-start(bf16[4096,128]{1,0:T(8,128)(2,1)} %query_hbm.3) | copy-start | bytes 3145732
  22.5 10.0 %copy-start = (bf16[2048,256]{1,0:T(8,128)(2,1)S(1)}, bf16[2048,256]{1,0:T(8,128)(2,1)}, u32[]{:S(2)}) copy-start(bf16[2048,256]{1,0:T(8,128)(2,1)} %embed_hbm.1) | copy-start | bytes 3145732
  22.5 10.0 %copy-start.2 = (bf16[256,256]{1,0:T(8,128)(2,1)S(1)}, bf16[256,256]{1,0:T(8,128)(2,1)}, u32[]{:S(2)}) copy-start(bf16[256,256]{1,0:T(8,128)(2,1)} %weight.1) | copy-start | bytes 393220
  22.5 8.9 %collective-permute-start = (bf16[1280,128]{1,0:T(8,128)(2,1)S(1)}, bf16[1280,128]{1,0:T(8,128)(2,1)S(1)}, u32[]{:S(2)}, u32[]{:S(2)}) collective-permute-start(bf16[1280,128]{1,0:T(8,128)(2,1)S(1)} %get-tuple-element.10), channel_id=1, source_target_pairs={{0,1},{1,0},{2,3},{3,2},{4,5},{5,4},{6,7},{7,6},{8,9},{9,8},{10,11... | collective-permute-start | bytes 983048 | tf_op jit(solution)/shard_map/ppermute | solution.py:249
  30.9 1.6 %collective-permute-start.3 = (bf16[768,128]{1,0:T(8,128)(2,1)S(1)}, bf16[768,128]{1,0:T(8,128)(2,1)S(1)}, u32[]{:S(2)}, u32[]{:S(2)}) collective-permute-start(bf16[768,128]{1,0:T(8,128)(2,1)S(1)} %get-tuple-element.12), channel_id=1, source_target_pairs={{0,1},{1,0},{2,3},{3,2},{4,5},{5,4},{6,7},{7,6},{8,9},{9,8},{10,11... | collective-permute-start | bytes 589832 | tf_op jit(solution)/shard_map/ppermute | solution.py:265
  32.5 0.7 %copy-start.3 = (f32[256]{0:T(256)S(1)}, f32[256]{0:T(256)}, u32[]{:S(2)}) copy-start(f32[256]{0:T(256)} %param.13) | copy-start | bytes 3076

commit v3 on v2

--- a/solution.py
+++ b/solution.py
@@ -78,13 +78,14 @@
 
 
 def attend(first, count, offset, blocks, unroll, bands, query, slots, load_window, load_values, out):
-    starts, counts = bands
+    starts, counts, vblocks, vblocks_all = bands
+    home = lax.axis_index("loop") * vblocks
 
     def query_rows(b):
         return query[pl.ds(pl.multiple_of((first + b) * QB, QB), QB), :]
 
     def place(b):
-        start = starts[first + b] - offset
+        start = lax.rem(starts[first + b] - home + REACH + vblocks_all, vblocks_all) - offset
         return start, jnp.minimum(jnp.maximum(start, 0), blocks - MOST)
 
     slots[0][...] = scores_of(query_rows(0), place(0)[1], load_window)
@@ -115,62 +116,109 @@
     return pl.ds(pl.multiple_of(i * size, size), count * size)
 
 
-def mid_kernel(starts, counts, query_hbm, kv, other, own, query, values_t, score_a, score_b, sem):
-    copy = pltpu.make_async_copy(query_hbm, query, sem)
-    copy.start()
+def load_bands(starts_hbm, counts_hbm, starts, counts, sems):
+    copies = [
+        pltpu.make_async_copy(starts_hbm, starts, sems.at[0]),
+        pltpu.make_async_copy(counts_hbm, counts, sems.at[1]),
+    ]
+    for copy in copies:
+        copy.start()
+    return copies
+
+
+def mid_attend(side, starts, counts, query, kv, values_t, slots, vblocks_all, out):
     vblocks, qblocks = kv.shape[0] // VB, query.shape[0] // QB
     edge_q = qblocks // vblocks * REACH
     mid_q = qblocks // 2 - edge_q
+    attend(
+        edge_q + side * mid_q, mid_q, REACH, vblocks, 5, (starts, counts, vblocks, vblocks_all),
+        query, slots, lambda begin: kv[rows_of(begin, MOST, VB), :],
+        lambda block: values_t[block], out,
+    )
+
+
+def other_mid_kernel(
+    vblocks_all, starts_hbm, counts_hbm, query_hbm, kv_hbm, out, values_t,
+    starts, counts, query, kv, score_a, score_b, sems,
+):
+    vblocks = kv.shape[0] // VB
+    cuts = 4
+    step = vblocks // cuts
+    pieces = [
+        pltpu.make_async_copy(
+            kv_hbm.at[pl.ds(c * step * VB, step * VB)],
+            kv.at[pl.ds(c * step * VB, step * VB)],
+            sems.at[2 + c],
+        )
+        for c in range(cuts)
+    ]
+    for piece in pieces:
+        piece.start()
+    bands = load_bands(starts_hbm, counts_hbm, starts, counts, sems)
+    copy = pltpu.make_async_copy(
+        query_hbm,
+        query,
+        sems.at[2 + cuts],
+    )
+    copy.start()
+    for c, piece in enumerate(pieces):
+        piece.wait()
+        prepare(
+            step, lambda i: kv[rows_of(c * step + i, 1, VB), :],
+            values_t.at[pl.ds(c * step, step)],
+        )
+    for band in bands:
+        band.wait()
+    copy.wait()
+    mid_attend(
+        1 - lax.axis_index("head"), starts, counts, query, kv, values_t, (score_a, score_b),
+        vblocks_all, out,
+    )
+
+
+def own_mid_kernel(
+    vblocks_all, starts_hbm, counts_hbm, query, kv, values_t, out,
+    starts, counts, score_a, score_b, sems,
+):
+    for band in load_bands(starts_hbm, counts_hbm, starts, counts, sems):
+        band.wait()
+    mid_attend(
+        lax.axis_index("head"), starts, counts, query, kv, values_t, (score_a, score_b),
+        vblocks_all, out,
+    )
+
+
+def edge_kernel(
+    vblocks_all, own, starts_hbm, counts_hbm, query, kv, left, right, out,
+    starts, counts, kv_edge, values_t, score_a, score_b, sems,
+):
+    bands = load_bands(starts_hbm, counts_hbm, starts, counts, sems)
     head = lax.axis_index("head")
-    prepare(vblocks, lambda i: kv[rows_of(i, 1, VB), :], values_t)
-    copy.wait()
-    for side, out in ((1 - head, other), (head, own)):
-        attend(
-            edge_q + side * mid_q, mid_q, REACH, vblocks, 5, (starts, counts), query,
-            (score_a, score_b), lambda begin: kv[rows_of(begin, MOST, VB), :],
-            lambda block: values_t[block], out,
-        )
-
-
-def edge_kernel(
-    starts, counts, query_hbm, kv_hbm, left, right, other, own,
-    query, kv_edge, values_t, score_a, score_b, sems,
-):
-    halo, rows = left.shape[0], kv_hbm.shape[0]
+    side = head if own else 1 - head
+    halo, rows = left.shape[0], kv.shape[0]
     vblocks, qblocks = rows // VB, query.shape[0] // QB
     edge_q = qblocks // vblocks * REACH
     near = 2 * halo
-    last = (qblocks - edge_q) * QB
-    copies = [
-        pltpu.make_async_copy(left, kv_edge.at[0, pl.ds(0, halo)], sems.at[0]),
-        pltpu.make_async_copy(
-            kv_hbm.at[pl.ds(0, near)], kv_edge.at[0, pl.ds(halo, near)], sems.at[1]
-        ),
-        pltpu.make_async_copy(
-            kv_hbm.at[pl.ds(rows - near, near)], kv_edge.at[1, pl.ds(0, near)], sems.at[2]
-        ),
-        pltpu.make_async_copy(right, kv_edge.at[1, pl.ds(near, halo)], sems.at[3]),
-        pltpu.make_async_copy(
-            query_hbm.at[pl.ds(0, edge_q * QB)], query.at[pl.ds(0, edge_q * QB)], sems.at[4]
-        ),
-        pltpu.make_async_copy(
-            query_hbm.at[pl.ds(last, edge_q * QB)], query.at[pl.ds(last, edge_q * QB)], sems.at[5]
-        ),
-    ]
-    for copy in copies:
-        copy.start()
-    for copy in copies:
-        copy.wait()
-    head = lax.axis_index("head")
-    for side in range(2):
-        prepare(3 * REACH, lambda i: kv_edge[side, rows_of(i, 1, VB), :], values_t.at[side])
-    for side, out in ((1 - head, other), (head, own)):
-        attend(
-            side * (qblocks - edge_q), edge_q, side * (vblocks - REACH), 3 * REACH, 3,
-            (starts, counts), query, (score_a, score_b),
-            lambda begin: kv_edge[side, rows_of(begin, MOST, VB), :],
-            lambda block: values_t[side, block], out,
-        )
+
+    @pl.when(side == 0)
+    def _():
+        kv_edge[:halo, :] = left[...]
+        kv_edge[halo:, :] = kv[:near, :]
+
+    @pl.when(side == 1)
+    def _():
+        kv_edge[:near, :] = kv[rows - near :, :]
+        kv_edge[near:, :] = right[...]
+
+    prepare(3 * REACH, lambda i: kv_edge[rows_of(i, 1, VB), :], values_t)
+    for band in bands:
+        band.wait()
+    attend(
+        side * (qblocks - edge_q), edge_q, side * (vblocks - REACH), 3 * REACH, 6,
+        (starts, counts, vblocks, vblocks_all), query, (score_a, score_b),
+        lambda begin: kv_edge[rows_of(begin, MOST, VB), :],
+        lambda block: values_t[block], out,
+    )
 
 
 def project_kernel(
@@ -182,7 +230,7 @@
     weights = jnp.concatenate(
         [weight[rows_of(head, 1, VB), :], weight[rows_of(1 - head, 1, VB), :]], axis=0
     )
-    gains = gain[...]
+    gains = gain[...].reshape(1, -1)
     tile = 256
     copy.wait()
     sends = []
@@ -212,57 +260,79 @@
 
 def local(query_embed, query_heads, voxel_kv, band_start, band_count, out_weight, norm_gain):
     loop_size = lax.axis_size("loop")
-    me = lax.axis_index("loop")
     vblocks, qblocks = voxel_kv.shape[0] // VB, query_heads.shape[0] // QB
     halo = REACH * VB
     edge_rows = qblocks // vblocks * REACH * QB
     mid_rows = query_heads.shape[0] // 2 - edge_rows
     vmem = pl.BlockSpec(memory_space=pltpu.VMEM)
-    smem = pl.BlockSpec(memory_space=pltpu.SMEM)
     hbm = pl.BlockSpec(memory_space=pl.ANY)
+    pinned = pl.BlockSpec(memory_space=pltpu.HBM)
     ring = range(loop_size)
-    right = lax.ppermute(voxel_kv[:halo], "loop", [(s, (s - 1) % loop_size) for s in ring])
-    left = lax.ppermute(voxel_kv[-halo:], "loop", [(s, (s + 1) % loop_size) for s in ring])
-    starts = jnp.mod(band_start - me * vblocks + REACH, vblocks * loop_size)
-    params = pltpu.CompilerParams(vmem_limit_bytes=40 * 2**20)
-    query_scratch = pltpu.VMEM(query_heads.shape, BF16)
+    vblocks_all = vblocks * loop_size
+    params = pltpu.CompilerParams(vmem_limit_bytes=32 * 2**20)
     slots = [pltpu.VMEM((MOST * VB, 4 * QB), F32)] * 2
+    band_scratch = [pltpu.SMEM(band_start.shape, jnp.int32)] * 2
+    values_shape = (vblocks, VB + 16, VB)
 
     def cost(rows):
         return pl.CostEstimate(
             flops=rows * 2**19, bytes_accessed=rows * 2**10, transcendentals=rows * 2**11
         )
 
-    other_mid, own_mid = pl.pallas_call(
-        mid_kernel,
-        out_shape=[jax.ShapeDtypeStruct((mid_rows, VB), BF16)] * 2,
-        in_specs=[smem, smem, hbm, vmem],
+    other_mid, values_t = pl.pallas_call(
+        functools.partial(other_mid_kernel, vblocks_all),
+        out_shape=[
+            jax.ShapeDtypeStruct((mid_rows, VB), BF16),
+            jax.ShapeDtypeStruct(values_shape, BF16),
+        ],
+        in_specs=[pinned] * 4,
         out_specs=[vmem, vmem],
         scratch_shapes=[
-            query_scratch, pltpu.VMEM((vblocks, VB + 16, VB), BF16), *slots,
-            pltpu.SemaphoreType.DMA,
+            *band_scratch, pltpu.VMEM(query_heads.shape, BF16), pltpu.VMEM(voxel_kv.shape, BF16),
+            *slots, pltpu.SemaphoreType.DMA((7,)),
         ],
         compiler_params=params,
-        cost_estimate=cost(2 * mid_rows),
-    )(starts, band_count, query_heads, voxel_kv)
+        cost_estimate=cost(mid_rows),
+    )(band_start, band_count, query_heads, voxel_kv)
     swap = [(0, 1), (1, 0)]
+    first, last, other_mid = lax.optimization_barrier(
+        (voxel_kv[:halo], voxel_kv[-halo:], other_mid)
+    )
+    right = lax.ppermute(first, "loop", [(s, (s - 1) % loop_size) for s in ring])
+    left = lax.ppermute(last, "loop", [(s, (s + 1) % loop_size) for s in ring])
     got_mid = lax.ppermute(other_mid, "head", swap)
-    other_edge, own_edge = pl.pallas_call(
-        edge_kernel,
-        out_shape=[jax.ShapeDtypeStruct((edge_rows, VB), BF16)] * 2,
-        in_specs=[smem, smem, hbm, hbm, hbm, hbm],
-        out_specs=[vmem, vmem],
-        scratch_shapes=[
-            query_scratch,
-            pltpu.VMEM((2, 3 * halo, voxel_kv.shape[1]), BF16),
-            pltpu.VMEM((2, 3 * REACH, VB + 16, VB), BF16),
-            *slots,
-            pltpu.SemaphoreType.DMA((6,)),
-        ],
+    own_mid = pl.pallas_call(
+        functools.partial(own_mid_kernel, vblocks_all),
+        out_shape=jax.ShapeDtypeStruct((mid_rows, VB), BF16),
+        in_specs=[pinned, pinned, vmem, vmem, vmem],
+        out_specs=vmem,
+        scratch_shapes=[*band_scratch, *slots, pltpu.SemaphoreType.DMA((2,))],
         compiler_params=params,
-        cost_estimate=cost(2 * edge_rows),
-    )(starts, band_count, query_heads, voxel_kv, left, right)
+        cost_estimate=cost(mid_rows),
+    )(band_start, band_count, query_heads, voxel_kv, values_t)
+    left, right, own_mid = lax.optimization_barrier((left, right, own_mid))
+
+    def edge(own, left):
+        return pl.pallas_call(
+            functools.partial(edge_kernel, vblocks_all, own),
+            out_shape=jax.ShapeDtypeStruct((edge_rows, VB), BF16),
+            in_specs=[pinned, pinned, vmem, vmem, vmem, vmem],
+            out_specs=vmem,
+            scratch_shapes=[
+                *band_scratch,
+                pltpu.VMEM((3 * halo, voxel_kv.shape[1]), BF16),
+                pltpu.VMEM((3 * REACH, VB + 16, VB), BF16),
+                *slots,
+                pltpu.SemaphoreType.DMA((2,)),
+            ],
+            compiler_params=params,
+            cost_estimate=cost(edge_rows),
+        )(band_start, band_count, query_heads, voxel_kv, left, right)
+
+    other_edge = edge(False, left)
+    other_edge, left = lax.optimization_barrier((other_edge, left))
     got_edge = lax.ppermute(other_edge, "head", swap)
+    own_edge = edge(True, left)
     return pl.pallas_call(
         project_kernel,
         out_shape=jax.ShapeDtypeStruct(query_embed.shape, BF16),
@@ -274,7 +344,7 @@
             pltpu.SemaphoreType.DMA((1 + query_embed.shape[0] // 256,)),
         ],
         compiler_params=params,
-    )(own_mid, got_mid, own_edge, got_edge, query_embed, out_weight, norm_gain.reshape(1, -1))
+    )(own_mid, got_mid, own_edge, got_edge, query_embed, out_weight, norm_gain)
 
 
 def solution(mesh):

time: 35.2 us -> 31.4 us (0.89)
  local copies, waits for them, and re-layouts: 5.48 us -> 3.54 us
  Pallas kernels: 20.7 us -> 19.5 us
  starting transfers between devices: 7.6 us -> 7.13 us
    unnamed x14, local copies, waits for them, and re-layouts: 4.43 us -> 2.47 us
    pallas_call x2 -> x4, Pallas kernels: 18.9 us -> 17.7 us  [the longest x2 6.72 us: edge(): pl.pallas_call(functools.partial(edge_kernel, vblocks_all, own), out_shap...]
    ppermute x1, waiting for transfers between devices: 1.07 us -> 0.01 us  [local(): got_edge = lax.ppermute(other_edge, 'head', swap)]
    ppermute x2, waiting for transfers between devices: 0.01 us -> 0.82 us  [the longest x1 0.82 us: local(): lax.ppermute(first, 'loop', [(s, (s - 1) % loop_size) for s in ring])]
    ppermute x1, starting transfers between devices: 0.54 us -> 0.07 us  [local(): got_edge = lax.ppermute(other_edge, 'head', swap)]
  transfers between devices with their start and end apart: 4 -> 4, of which waited for: 1 -> 1; matrix products, arithmetic and copies ran while one was open for 0% -> 0% of each run, Pallas kernels for 54% -> 39%
where the time goes in v3:
time: 31.4 us; the launch traced here: 31.1 us
  Pallas kernels  19.5 us (62%)
  starting transfers between devices  7.13 us (23%)
  local copies, waits for them, and re-layouts  3.54 us (11%)
  waiting for transfers between devices  0.83 us (3%)
    pallas_call x2, Pallas kernels, edge(): pl.pallas_call(functools.partial(edge_kernel, vblocks_all, own), out_shap...  6.72 us
    pallas_call x1, Pallas kernels, local(): pl.pallas_call(functools.partial(other_mid_kernel, vblocks_all), out_shap...  5.54 us
    pallas_call x1, Pallas kernels, local(): pl.pallas_call(functools.partial(own_mid_kernel, vblocks_all), out_shape=...  5.42 us
    ppermute x1, starting transfers between devices, local(): lax.ppermute(first, 'loop', [(s, (s - 1) % loop_size) for s in ring])  4.04 us
    ppermute x1, starting transfers between devices, local(): left = lax.ppermute(last, 'loop', [(s, (s + 1) % loop_size) for s in ring])  3.02 us
    unnamed x14, local copies, waits for them, and re-layouts  2.47 us
    pallas_call x1, Pallas kernels, local(): pl.pallas_call(project_kernel, out_shape=jax.ShapeDtypeStruct(query_embed...  1.78 us
    slice x1, local copies, waits for them, and re-layouts, local(): voxel_kv[-halo:]  1.07 us
  transfers between devices with their start and end apart: 4, of which 1 were waited for; matrix products, arithmetic and copies ran while one was open for 0% of the time, Pallas kernels for 39%

profile of v3, /device:TPU:0, one launch (start us, length us, event | category | flops | bytes accessed | tf_op | source)
XLA Modules:
  0.0 31.1 jit_solution(87207047207868822)
XLA Ops:
  0.0 0.0 copy-start.6
  0.0 0.0 copy-start.5
  0.0 1.1 %fusion = (bf16[384,256]{1,0:T(8,128)(2,1)S(1)}, bf16[384,256]{1,0:T(8,128)(2,1)S(1)}) fusion(bf16[2048,256]{1,0:T(8,128)(2,1)} %kv.5), kind=kLoop, calls=%fused_computation | loop fusion | bytes 786432 | tf_op jit(solution)/shard_map/slice | solution.py:299
  1.1 0.0 copy-done.6
  1.1 0.0 copy-done.5
  1.1 0.0 copy-start.1
  1.1 1.2 %copy-done.1 = bf16[2048,256]{1,0:T(8,128)(2,1)S(1)} copy-done((bf16[2048,256]{1,0:T(8,128)(2,1)S(1)}, bf16[2048,256]{1,0:T(8,128)(2,1)}, u32[]{:S(2)}) %copy-start.1) | copy-done | bytes 1048600
  2.3 0.0 copy-start.4
  2.3 1.2 %copy-done.4 = bf16[4096,128]{1,0:T(8,128)(2,1)S(1)} copy-done((bf16[4096,128]{1,0:T(8,128)(2,1)S(1)}, bf16[4096,128]{1,0:T(8,128)(2,1)}, u32[]{:S(2)}) %copy-start.4) | copy-done | bytes 1048600
  3.6 5.5 %shard_map.73 = (bf16[1280,128]{1,0:T(8,128)(2,1)S(1)}, bf16[16,144,128]{2,1,0:T(8,128)(2,1)S(1)}) custom-call(s32[64]{0:T(128)S(1)} %copy-done.5, s32[64]{0:T(128)S(1)} %copy-done.6, bf16[4096,128]{1,0:T(8,128)(2,1)S(1)} %copy-done.4, bf16[2048,256]{1,0:T(8,128)(2,1)S(1)} %copy-done.1), custom_call_target="tpu_custom_call" | custom-call | flops 671088640 | bytes 1310720 | tf_op jit(solution)/shard_map/pallas_call | solution.py:282
  9.1 3.0 %collective-permute-start = (bf16[384,256]{1,0:T(8,128)(2,1)S(1)}, bf16[384,256]{1,0:T(8,128)(2,1)S(1)}, u32[]{:S(2)}, u32[]{:S(2)}) collective-permute-start(bf16[384,256]{1,0:T(8,128)(2,1)S(1)} %get-tuple-element.16), channel_id=1, source_target_pairs={{0,2},{2,4},{4,6},{6,8},{8,10},{10,12},{12,14},{14,16},{16,18},{18... | collective-permute-start | bytes 589832 | tf_op jit(solution)/shard_map/ppermute | solution.py:302
  12.1 4.0 %collective-permute-start.1 = (bf16[384,256]{1,0:T(8,128)(2,1)S(1)}, bf16[384,256]{1,0:T(8,128)(2,1)S(1)}, u32[]{:S(2)}, u32[]{:S(2)}) collective-permute-start(bf16[384,256]{1,0:T(8,128)(2,1)S(1)} %get-tuple-element.17), channel_id=1, source_target_pairs={{0,30},{2,0},{4,2},{6,4},{8,6},{10,8},{12,10},{14,12},{16,14},{18,... | collective-permute-start | bytes 589832 | tf_op jit(solution)/shard_map/ppermute | solution.py:301
  16.2 0.0 collective-permute-start.2
  16.2 5.4 %shard_map.74.own_mid = bf16[1280,128]{1,0:T(8,128)(2,1)S(1)} custom-call(s32[64]{0:T(128)S(1)} %copy-done.5, s32[64]{0:T(128)S(1)} %copy-done.6, bf16[4096,128]{1,0:T(8,128)(2,1)S(1)} %copy-done.4, bf16[2048,256]{1,0:T(8,128)(2,1)S(1)} %copy-done.1, bf16[16,144,128]{2,1,0:T(8,128)(2,1)S(1)} %get-tuple-element.18.values_t), custom_call_target="tpu_custom_call" | custom-call | flops 671088640 | bytes 1310720 | tf_op jit(solution)/shard_map/pallas_call | solution.py:304
  21.6 0.0 collective-permute-done.left
  21.6 0.8 %collective-permute-done.1.right = bf16[384,256]{1,0:T(8,128)(2,1)S(1)} collective-permute-done((bf16[384,256]{1,0:T(8,128)(2,1)S(1)}, bf16[384,256]{1,0:T(8,128)(2,1)S(1)}, u32[]{:S(2)}, u32[]{:S(2)}) %collective-permute-start.1) | collective-permute-done | bytes 196640 | tf_op jit(solution)/shard_map/ppermute | solution.py:301
  22.4 3.4 %shard_map.75 = bf16[768,128]{1,0:T(8,128)(2,1)S(1)} custom-call(s32[64]{0:T(128)S(1)} %copy-done.5, s32[64]{0:T(128)S(1)} %copy-done.6, bf16[4096,128]{1,0:T(8,128)(2,1)S(1)} %copy-done.4, bf16[2048,256]{1,0:T(8,128)(2,1)S(1)} %copy-done.1, bf16[384,256]{1,0:T(8,128)(2,1)S(1)} %collective-permute-done.left, bf16[384,256]{1,0:T(8,128)(2,1)S(1)} %collective-permute-done.1.right), custom_call_target="tpu_custom_call" | custom-call | flops 402653184 | bytes 786432 | tf_op jit(solution)/shard_map/pallas_call | solution.py:316
  25.8 0.0 copy-start
  25.8 0.0 copy-start.2
  25.8 0.0 copy-start.3
  25.8 0.1 collective-permute-start.3
  25.9 3.4 %shard_map.76.own_edge = bf16[768,128]{1,0:T(8,128)(2,1)S(1)} custom-call(s32[64]{0:T(128)S(1)} %copy-done.5, s32[64]{0:T(128)S(1)} %copy-done.6, bf16[4096,128]{1,0:T(8,128)(2,1)S(1)} %copy-done.4, bf16[2048,256]{1,0:T(8,128)(2,1)S(1)} %copy-done.1, bf16[384,256]{1,0:T(8,128)(2,1)S(1)} %collective-permute-done.left, ...), custom_call_target="tpu_custom_call" | custom-call | flops 402653184 | bytes 786432 | tf_op jit(solution)/shard_map/pallas_call | solution.py:316
  29.3 0.0 collective-permute-done.2.got_mid
  29.3 0.0 collective-permute-done.3.got_edge
  29.3 0.0 copy-done
  29.3 0.0 copy-done.2
  29.3 0.0 copy-done.3
  29.3 1.8 %shard_map.77 = bf16[2048,256]{1,0:T(8,128)(2,1)} custom-call(bf16[1280,128]{1,0:T(8,128)(2,1)S(1)} %shard_map.74.own_mid, bf16[1280,128]{1,0:T(8,128)(2,1)S(1)} %collective-permute-done.2.got_mid, bf16[768,128]{1,0:T(8,128)(2,1)S(1)} %shard_map.76.own_edge, bf16[768,128]{1,0:T(8,128)(2,1)S(1)} %collective-permute-done.3.got_edge, ...), custom_call_target="tpu_custom_call" | custom-call | tf_op jit(solution)/shard_map/pallas_call | solution.py:336
Async XLA Ops:
  0.0 1.1 %copy-start.6 = (s32[64]{0:T(128)S(1)}, s32[64]{0:T(128)}, u32[]{:S(2)}) copy-start(s32[64]{0:T(128)} %counts_hbm.7) | copy-start | bytes 772
  0.0 1.1 %copy-start.5 = (s32[64]{0:T(128)S(1)}, s32[64]{0:T(128)}, u32[]{:S(2)}) copy-start(s32[64]{0:T(128)} %starts_hbm.7) | copy-start | bytes 772
  1.1 1.2 %copy-start.1 = (bf16[2048,256]{1,0:T(8,128)(2,1)S(1)}, bf16[2048,256]{1,0:T(8,128)(2,1)}, u32[]{:S(2)}) copy-start(bf16[2048,256]{1,0:T(8,128)(2,1)} %kv.5) | copy-start | bytes 3145732
  2.3 1.2 %copy-start.4 = (bf16[4096,128]{1,0:T(8,128)(2,1)S(1)}, bf16[4096,128]{1,0:T(8,128)(2,1)}, u32[]{:S(2)}) copy-start(bf16[4096,128]{1,0:T(8,128)(2,1)} %query.5) | copy-start | bytes 3145732
  9.1 12.5 %collective-permute-start = (bf16[384,256]{1,0:T(8,128)(2,1)S(1)}, bf16[384,256]{1,0:T(8,128)(2,1)S(1)}, u32[]{:S(2)}, u32[]{:S(2)}) collective-permute-start(bf16[384,256]{1,0:T(8,128)(2,1)S(1)} %get-tuple-element.16), channel_id=1, source_target_pairs={{0,2},{2,4},{4,6},{6,8},{8,10},{10,12},{12,14},{14,16},{16,18},{18... | collective-permute-start | bytes 589832 | tf_op jit(solution)/shard_map/ppermute | solution.py:302
  12.1 10.3 %collective-permute-start.1 = (bf16[384,256]{1,0:T(8,128)(2,1)S(1)}, bf16[384,256]{1,0:T(8,128)(2,1)S(1)}, u32[]{:S(2)}, u32[]{:S(2)}) collective-permute-start(bf16[384,256]{1,0:T(8,128)(2,1)S(1)} %get-tuple-element.17), channel_id=1, source_target_pairs={{0,30},{2,0},{4,2},{6,4},{8,6},{10,8},{12,10},{14,12},{16,14},{18,... | collective-permute-start | bytes 589832 | tf_op jit(solution)/shard_map/ppermute | solution.py:301
  16.2 13.1 %collective-permute-start.2 = (bf16[1280,128]{1,0:T(8,128)(2,1)S(1)}, bf16[1280,128]{1,0:T(8,128)(2,1)S(1)}, u32[]{:S(2)}, u32[]{:S(2)}) collective-permute-start(bf16[1280,128]{1,0:T(8,128)(2,1)S(1)} %get-tuple-element.20), channel_id=1, source_target_pairs={{0,1},{1,0},{2,3},{3,2},{4,5},{5,4},{6,7},{7,6},{8,9},{9,8},{10,11... | collective-permute-start | bytes 983048 | tf_op jit(solution)/shard_map/ppermute | solution.py:303
  25.8 3.5 %copy-start = (bf16[2048,256]{1,0:T(8,128)(2,1)S(1)}, bf16[2048,256]{1,0:T(8,128)(2,1)}, u32[]{:S(2)}) copy-start(bf16[2048,256]{1,0:T(8,128)(2,1)} %embed_hbm.1) | copy-start | bytes 3145732
  25.8 3.5 %copy-start.2 = (bf16[256,256]{1,0:T(8,128)(2,1)S(1)}, bf16[256,256]{1,0:T(8,128)(2,1)}, u32[]{:S(2)}) copy-start(bf16[256,256]{1,0:T(8,128)(2,1)} %weight.1) | copy-start | bytes 393220
  25.8 3.5 %copy-start.3 = (f32[256]{0:T(256)S(1)}, f32[256]{0:T(256)}, u32[]{:S(2)}) copy-start(f32[256]{0:T(256)} %gain.1) | copy-start | bytes 3076
  25.8 3.5 %collective-permute-start.3 = (bf16[768,128]{1,0:T(8,128)(2,1)S(1)}, bf16[768,128]{1,0:T(8,128)(2,1)S(1)}, u32[]{:S(2)}, u32[]{:S(2)}) collective-permute-start(bf16[768,128]{1,0:T(8,128)(2,1)S(1)} %shard_map.75), channel_id=1, source_target_pairs={{0,1},{1,0},{2,3},{3,2},{4,5},{5,4},{6,7},{7,6},{8,9},{9,8},{10,11... | collective-permute-start | bytes 589832 | tf_op jit(solution)/shard_map/ppermute | solution.py:334

commit v4 on v3

--- a/solution.py
+++ b/solution.py
@@ -131,45 +131,20 @@
     edge_q = qblocks // vblocks * REACH
     mid_q = qblocks // 2 - edge_q
     attend(
-        edge_q + side * mid_q, mid_q, REACH, vblocks, 5, (starts, counts, vblocks, vblocks_all),
+        edge_q + side * mid_q, mid_q, REACH, vblocks, 10, (starts, counts, vblocks, vblocks_all),
         query, slots, lambda begin: kv[rows_of(begin, MOST, VB), :],
         lambda block: values_t[block], out,
     )
 
 
 def other_mid_kernel(
-    vblocks_all, starts_hbm, counts_hbm, query_hbm, kv_hbm, out, values_t,
-    starts, counts, query, kv, score_a, score_b, sems,
+    vblocks_all, starts_hbm, counts_hbm, query, kv, out, values_t,
+    starts, counts, score_a, score_b, sems,
 ):
-    vblocks = kv.shape[0] // VB
-    cuts = 4
-    step = vblocks // cuts
-    pieces = [
-        pltpu.make_async_copy(
-            kv_hbm.at[pl.ds(c * step * VB, step * VB)],
-            kv.at[pl.ds(c * step * VB, step * VB)],
-            sems.at[2 + c],
-        )
-        for c in range(cuts)
-    ]
-    for piece in pieces:
-        piece.start()
-    bands = load_bands(starts_hbm, counts_hbm, starts, counts, sems)
-    copy = pltpu.make_async_copy(
-        query_hbm,
-        query,
-        sems.at[2 + cuts],
-    )
-    copy.start()
-    for c, piece in enumerate(pieces):
-        piece.wait()
-        prepare(
-            step, lambda i: kv[rows_of(c * step + i, 1, VB), :],
-            values_t.at[pl.ds(c * step, step)],
-        )
-    for band in bands:
-        band.wait()
-    copy.wait()
+    copies = load_bands(starts_hbm, counts_hbm, starts, counts, sems)
+    prepare(kv.shape[0] // VB, lambda i: kv[rows_of(i, 1, VB), :], values_t)
+    for copy in copies:
+        copy.wait()
     mid_attend(
         1 - lax.axis_index("head"), starts, counts, query, kv, values_t, (score_a, score_b),
         vblocks_all, out,
@@ -285,12 +260,9 @@
             jax.ShapeDtypeStruct((mid_rows, VB), BF16),
             jax.ShapeDtypeStruct(values_shape, BF16),
         ],
-        in_specs=[pinned] * 4,
-        out_specs=[vmem, vmem],
-        scratch_shapes=[
-            *band_scratch, pltpu.VMEM(query_heads.shape, BF16), pltpu.VMEM(voxel_kv.shape, BF16),
-            *slots, pltpu.SemaphoreType.DMA((7,)),
-        ],
+        in_specs=[pinned, pinned, vmem, vmem],
+        out_specs=[vmem] * 2,
+        scratch_shapes=[*band_scratch, *slots, pltpu.SemaphoreType.DMA((2,))],
         compiler_params=params,
         cost_estimate=cost(mid_rows),
     )(band_start, band_count, query_heads, voxel_kv)

time: 31.4 us -> 31.2 us (level)
  Pallas kernels: 19.5 us -> 18.8 us
    pallas_call x1, Pallas kernels: 5.54 us -> 5.17 us  [local(): pl.pallas_call(functools.partial(other_mid_kernel, vblocks_all), out_shap...]
  transfers between devices with their start and end apart: 4 -> 4, of which waited for: 1 -> 1; matrix products, arithmetic and copies ran while one was open for 0% -> 0% of each run, Pallas kernels for 39% -> 38%
where the time goes in v4:
time: 31.2 us; the launch traced here: 30.9 us
  Pallas kernels  18.8 us (60%)
  starting transfers between devices  7.13 us (23%)
  local copies, waits for them, and re-layouts  3.54 us (11%)
  waiting for transfers between devices  1.1 us (4%)
    pallas_call x2, Pallas kernels, edge(): pl.pallas_call(functools.partial(edge_kernel, vblocks_all, own), out_shap...  6.72 us
    pallas_call x1, Pallas kernels, local(): pl.pallas_call(functools.partial(other_mid_kernel, vblocks_all), out_shap...  5.17 us
    pallas_call x1, Pallas kernels, local(): pl.pallas_call(functools.partial(own_mid_kernel, vblocks_all), out_shape=...  5.16 us
    ppermute x1, starting transfers between devices, local(): lax.ppermute(first, 'loop', [(s, (s - 1) % loop_size) for s in ring])  4.06 us
    ppermute x1, starting transfers between devices, local(): left = lax.ppermute(last, 'loop', [(s, (s + 1) % loop_size) for s in ring])  2.99 us
    unnamed x14, local copies, waits for them, and re-layouts  2.47 us
    pallas_call x1, Pallas kernels, local(): pl.pallas_call(project_kernel, out_shape=jax.ShapeDtypeStruct(query_embed...  1.78 us
    ppermute x1, waiting for transfers between devices, local(): lax.ppermute(first, 'loop', [(s, (s - 1) % loop_size) for s in ring])  1.09 us
  transfers between devices with their start and end apart: 4, of which 1 were waited for; matrix products, arithmetic and copies ran while one was open for 0% of the time, Pallas kernels for 38%

profile of v4, /device:TPU:0, one launch (start us, length us, event | category | flops | bytes accessed | tf_op | source)
XLA Modules:
  0.0 30.9 jit_solution(14981457010346155833)
XLA Ops:
  0.0 0.0 copy-start.6
  0.0 0.0 copy-start.5
  0.0 1.1 %fusion = (bf16[384,256]{1,0:T(8,128)(2,1)S(1)}, bf16[384,256]{1,0:T(8,128)(2,1)S(1)}) fusion(bf16[2048,256]{1,0:T(8,128)(2,1)} %kv.7), kind=kLoop, calls=%fused_computation | loop fusion | bytes 786432 | tf_op jit(solution)/shard_map/slice | solution.py:271
  1.1 0.0 copy-done.6
  1.1 0.0 copy-done.5
  1.1 0.0 copy-start.1
  1.1 1.2 %copy-done.1 = bf16[2048,256]{1,0:T(8,128)(2,1)S(1)} copy-done((bf16[2048,256]{1,0:T(8,128)(2,1)S(1)}, bf16[2048,256]{1,0:T(8,128)(2,1)}, u32[]{:S(2)}) %copy-start.1) | copy-done | bytes 1048600
  2.3 0.0 copy-start.4
  2.3 1.2 %copy-done.4 = bf16[4096,128]{1,0:T(8,128)(2,1)S(1)} copy-done((bf16[4096,128]{1,0:T(8,128)(2,1)S(1)}, bf16[4096,128]{1,0:T(8,128)(2,1)}, u32[]{:S(2)}) %copy-start.4) | copy-done | bytes 1048600
  3.6 5.2 %shard_map.73 = (bf16[1280,128]{1,0:T(8,128)(2,1)S(1)}, bf16[16,144,128]{2,1,0:T(8,128)(2,1)S(1)}) custom-call(s32[64]{0:T(128)S(1)} %copy-done.5, s32[64]{0:T(128)S(1)} %copy-done.6, bf16[4096,128]{1,0:T(8,128)(2,1)S(1)} %copy-done.4, bf16[2048,256]{1,0:T(8,128)(2,1)S(1)} %copy-done.1), custom_call_target="tpu_custom_call" | custom-call | flops 671088640 | bytes 1310720 | tf_op jit(solution)/shard_map/pallas_call | solution.py:257
  8.7 3.0 %collective-permute-start = (bf16[384,256]{1,0:T(8,128)(2,1)S(1)}, bf16[384,256]{1,0:T(8,128)(2,1)S(1)}, u32[]{:S(2)}, u32[]{:S(2)}) collective-permute-start(bf16[384,256]{1,0:T(8,128)(2,1)S(1)} %get-tuple-element.16), channel_id=1, source_target_pairs={{0,2},{2,4},{4,6},{6,8},{8,10},{10,12},{12,14},{14,16},{16,18},{18... | collective-permute-start | bytes 589832 | tf_op jit(solution)/shard_map/ppermute | solution.py:274
  11.7 4.1 %collective-permute-start.1 = (bf16[384,256]{1,0:T(8,128)(2,1)S(1)}, bf16[384,256]{1,0:T(8,128)(2,1)S(1)}, u32[]{:S(2)}, u32[]{:S(2)}) collective-permute-start(bf16[384,256]{1,0:T(8,128)(2,1)S(1)} %get-tuple-element.17), channel_id=1, source_target_pairs={{0,30},{2,0},{4,2},{6,4},{8,6},{10,8},{12,10},{14,12},{16,14},{18,... | collective-permute-start | bytes 589832 | tf_op jit(solution)/shard_map/ppermute | solution.py:273
  15.8 0.0 collective-permute-start.2
  15.8 5.2 %shard_map.74.own_mid = bf16[1280,128]{1,0:T(8,128)(2,1)S(1)} custom-call(s32[64]{0:T(128)S(1)} %copy-done.5, s32[64]{0:T(128)S(1)} %copy-done.6, bf16[4096,128]{1,0:T(8,128)(2,1)S(1)} %copy-done.4, bf16[2048,256]{1,0:T(8,128)(2,1)S(1)} %copy-done.1, bf16[16,144,128]{2,1,0:T(8,128)(2,1)S(1)} %get-tuple-element.18.values_t), custom_call_target="tpu_custom_call" | custom-call | flops 671088640 | bytes 1310720 | tf_op jit(solution)/shard_map/pallas_call | solution.py:276
  21.0 0.0 collective-permute-done.left
  21.0 1.1 %collective-permute-done.1.right = bf16[384,256]{1,0:T(8,128)(2,1)S(1)} collective-permute-done((bf16[384,256]{1,0:T(8,128)(2,1)S(1)}, bf16[384,256]{1,0:T(8,128)(2,1)S(1)}, u32[]{:S(2)}, u32[]{:S(2)}) %collective-permute-start.1) | collective-permute-done | bytes 196640 | tf_op jit(solution)/shard_map/ppermute | solution.py:273
  22.1 3.4 %shard_map.75 = bf16[768,128]{1,0:T(8,128)(2,1)S(1)} custom-call(s32[64]{0:T(128)S(1)} %copy-done.5, s32[64]{0:T(128)S(1)} %copy-done.6, bf16[4096,128]{1,0:T(8,128)(2,1)S(1)} %copy-done.4, bf16[2048,256]{1,0:T(8,128)(2,1)S(1)} %copy-done.1, bf16[384,256]{1,0:T(8,128)(2,1)S(1)} %collective-permute-done.left, bf16[384,256]{1,0:T(8,128)(2,1)S(1)} %collective-permute-done.1.right), custom_call_target="tpu_custom_call" | custom-call | flops 402653184 | bytes 786432 | tf_op jit(solution)/shard_map/pallas_call | solution.py:288
  25.4 0.0 copy-start
  25.4 0.0 copy-start.2
  25.4 0.0 copy-start.3
  25.5 0.1 collective-permute-start.3
  25.5 3.4 %shard_map.76.own_edge = bf16[768,128]{1,0:T(8,128)(2,1)S(1)} custom-call(s32[64]{0:T(128)S(1)} %copy-done.5, s32[64]{0:T(128)S(1)} %copy-done.6, bf16[4096,128]{1,0:T(8,128)(2,1)S(1)} %copy-done.4, bf16[2048,256]{1,0:T(8,128)(2,1)S(1)} %copy-done.1, bf16[384,256]{1,0:T(8,128)(2,1)S(1)} %collective-permute-done.left, ...), custom_call_target="tpu_custom_call" | custom-call | flops 402653184 | bytes 786432 | tf_op jit(solution)/shard_map/pallas_call | solution.py:288
  28.9 0.0 collective-permute-done.2.got_mid
  28.9 0.0 collective-permute-done.3.got_edge
  28.9 0.0 copy-done
  28.9 0.0 copy-done.2
  28.9 0.0 copy-done.3
  29.0 1.8 %shard_map.77 = bf16[2048,256]{1,0:T(8,128)(2,1)} custom-call(bf16[1280,128]{1,0:T(8,128)(2,1)S(1)} %shard_map.74.own_mid, bf16[1280,128]{1,0:T(8,128)(2,1)S(1)} %collective-permute-done.2.got_mid, bf16[768,128]{1,0:T(8,128)(2,1)S(1)} %shard_map.76.own_edge, bf16[768,128]{1,0:T(8,128)(2,1)S(1)} %collective-permute-done.3.got_edge, ...), custom_call_target="tpu_custom_call" | custom-call | tf_op jit(solution)/shard_map/pallas_call | solution.py:308
Async XLA Ops:
  0.0 1.1 %copy-start.6 = (s32[64]{0:T(128)S(1)}, s32[64]{0:T(128)}, u32[]{:S(2)}) copy-start(s32[64]{0:T(128)} %counts_hbm.7) | copy-start | bytes 772
  0.0 1.1 %copy-start.5 = (s32[64]{0:T(128)S(1)}, s32[64]{0:T(128)}, u32[]{:S(2)}) copy-start(s32[64]{0:T(128)} %starts_hbm.7) | copy-start | bytes 772
  1.1 1.2 %copy-start.1 = (bf16[2048,256]{1,0:T(8,128)(2,1)S(1)}, bf16[2048,256]{1,0:T(8,128)(2,1)}, u32[]{:S(2)}) copy-start(bf16[2048,256]{1,0:T(8,128)(2,1)} %kv.7) | copy-start | bytes 3145732
  2.3 1.2 %copy-start.4 = (bf16[4096,128]{1,0:T(8,128)(2,1)S(1)}, bf16[4096,128]{1,0:T(8,128)(2,1)}, u32[]{:S(2)}) copy-start(bf16[4096,128]{1,0:T(8,128)(2,1)} %query.7) | copy-start | bytes 3145732
  8.7 12.2 %collective-permute-start = (bf16[384,256]{1,0:T(8,128)(2,1)S(1)}, bf16[384,256]{1,0:T(8,128)(2,1)S(1)}, u32[]{:S(2)}, u32[]{:S(2)}) collective-permute-start(bf16[384,256]{1,0:T(8,128)(2,1)S(1)} %get-tuple-element.16), channel_id=1, source_target_pairs={{0,2},{2,4},{4,6},{6,8},{8,10},{10,12},{12,14},{14,16},{16,18},{18... | collective-permute-start | bytes 589832 | tf_op jit(solution)/shard_map/ppermute | solution.py:274
  11.7 10.3 %collective-permute-start.1 = (bf16[384,256]{1,0:T(8,128)(2,1)S(1)}, bf16[384,256]{1,0:T(8,128)(2,1)S(1)}, u32[]{:S(2)}, u32[]{:S(2)}) collective-permute-start(bf16[384,256]{1,0:T(8,128)(2,1)S(1)} %get-tuple-element.17), channel_id=1, source_target_pairs={{0,30},{2,0},{4,2},{6,4},{8,6},{10,8},{12,10},{14,12},{16,14},{18,... | collective-permute-start | bytes 589832 | tf_op jit(solution)/shard_map/ppermute | solution.py:273
  15.8 13.1 %collective-permute-start.2 = (bf16[1280,128]{1,0:T(8,128)(2,1)S(1)}, bf16[1280,128]{1,0:T(8,128)(2,1)S(1)}, u32[]{:S(2)}, u32[]{:S(2)}) collective-permute-start(bf16[1280,128]{1,0:T(8,128)(2,1)S(1)} %get-tuple-element.20), channel_id=1, source_target_pairs={{0,1},{1,0},{2,3},{3,2},{4,5},{5,4},{6,7},{7,6},{8,9},{9,8},{10,11... | collective-permute-start | bytes 983048 | tf_op jit(solution)/shard_map/ppermute | solution.py:275
  25.4 3.5 %copy-start = (bf16[2048,256]{1,0:T(8,128)(2,1)S(1)}, bf16[2048,256]{1,0:T(8,128)(2,1)}, u32[]{:S(2)}) copy-start(bf16[2048,256]{1,0:T(8,128)(2,1)} %embed_hbm.1) | copy-start | bytes 3145732
  25.4 3.5 %copy-start.2 = (bf16[256,256]{1,0:T(8,128)(2,1)S(1)}, bf16[256,256]{1,0:T(8,128)(2,1)}, u32[]{:S(2)}) copy-start(bf16[256,256]{1,0:T(8,128)(2,1)} %weight.1) | copy-start | bytes 393220
  25.4 3.5 %copy-start.3 = (f32[256]{0:T(256)S(1)}, f32[256]{0:T(256)}, u32[]{:S(2)}) copy-start(f32[256]{0:T(256)} %gain.1) | copy-start | bytes 3076
  25.5 3.5 %collective-permute-start.3 = (bf16[768,128]{1,0:T(8,128)(2,1)S(1)}, bf16[768,128]{1,0:T(8,128)(2,1)S(1)}, u32[]{:S(2)}, u32[]{:S(2)}) collective-permute-start(bf16[768,128]{1,0:T(8,128)(2,1)S(1)} %shard_map.75), channel_id=1, source_target_pairs={{0,1},{1,0},{2,3},{3,2},{4,5},{5,4},{6,7},{7,6},{8,9},{9,8},{10,11... | collective-permute-start | bytes 589832 | tf_op jit(solution)/shard_map/ppermute | solution.py:306
